TPU v7x, 32 devices: a whole 2x2x4 slice. The times are simulated.
32 devices in a mesh: rep: 8 (over y, x, core), exp: 4 (over z).
Axes of the slice: x: 2, y: 2, z: 4, core: 2. Of those that a mesh axis runs over, the one named last changes fastest.
Arguments:
- hidden: bfloat16 [4096, 4096], P(('rep', 'exp')), may hold values from -6 to 6
- parents: int32 [4096], P(('rep', 'exp')), may hold values from 0 to 511
- routes: int32 [4096, 8], P(('rep', 'exp')), may hold values from 0 to 31, all different within a row; in each aligned block of 128 rows (0 to 127, 128 to 255, ...) at most 34 rows name the same one
- gates: float32 [4096, 8], P(('rep', 'exp')), may hold values from 0.05 to 1
- counts: int32 [32], P(('rep', 'exp')), may hold values from 64 to 128, as said below
- norm_gain: float32 [4096], replicated, may hold values from 0.1 to 1.9
- w_gate: bfloat16 [32, 4096, 768], P(('rep', 'exp')), may hold values from -0.09375 to 0.09375
- w_up: bfloat16 [32, 4096, 768], P(('rep', 'exp')), may hold values from -0.09375 to 0.09375
- w_down: bfloat16 [32, 768, 4096], P(('rep', 'exp')), may hold values from -0.21875 to 0.21875
Outputs:
- mixed: bfloat16 [4096, 4096], P(('rep', 'exp'))
Inputs may be any that keep to these rules, and one draw needn't show every extreme that they name: `routes`: in the rows of one device no expert is named more than 34 times. `counts`: some device has all of its rows live.
All inputs are finite; a program needn't handle non-finite values.
Results may differ from a plain program's by a relative error of at most 0.0071.
Values may be sent and summed in bfloat16 or wider, within the bound.
No kernel may reach another device: no remote copies, remote signals or barrier semaphores. Data moves between devices by JAX's collectives and lax.ppermute only.
A program may use at most 128 MiB of HBM per device.

v0:
```python
import functools

import jax
import jax.numpy as jnp
from jax import lax
from jax.experimental import pallas as pl
from jax.experimental.pallas import tpu as pltpu
from jax.sharding import PartitionSpec as P

IN_PARTS = (4, 7, 5)
OUT_PARTS = (4, 7, 5)
FACTS = 24
WEIGHT_ROW = 8
PARENT_ROW = 16
FITS_ROW = 17
BF16 = jnp.bfloat16


def dot(a, b):
    return jnp.dot(a, b, preferred_element_type=jnp.float32)


def dot_nt(a, b):
    return lax.dot_general(a, b, (((1,), (1,)), ((), ())), preferred_element_type=jnp.float32)


def dot_tn(a, b):
    return lax.dot_general(a, b, (((0,), (0,)), ((), ())), preferred_element_type=jnp.float32)


def round_up(value, unit):
    return -(-value // unit) * unit


def ring(value, axis, size, shift):
    if shift % size == 0:
        return value
    return lax.ppermute(value, axis, [(i, (i + shift) % size) for i in range(size)])


def flip(value, size, mask):
    if mask == 0:
        return value
    return lax.ppermute(value, "rep", [(i, i ^ mask) for i in range(size)])


def flat_iota(shape, dim):
    return lax.broadcasted_iota(jnp.int32, shape, dim)


def ones_where(condition):
    return jnp.where(condition, 1.0, 0.0).astype(BF16)


def any_hit(hits):
    return jnp.max(jnp.where(hits, 1.0, 0.0), axis=0, keepdims=True)


def parent_table(parent, group):
    return ones_where(flat_iota((group, group), 0) == parent.astype(jnp.int32))


def before_table(group, block):
    a = flat_iota((group, group), 0)
    b = flat_iota((group, group), 1)
    if block == group:
        return ones_where(a < b)
    low = b - lax.rem(b, block)
    return ones_where((a < b) & (a >= low))


def code_of(used, before):
    rank = dot(used.astype(BF16), before)
    return jnp.where(used > 0.5, rank + 1.0, 0.0)


def one_row(table, row):
    chosen = flat_iota(table.shape, 0) == row
    return jnp.sum(jnp.where(chosen, table, 0.0), axis=0, keepdims=True)


def slots_of(code, slots):
    return ones_where(flat_iota((slots, code.shape[1]), 0) + 1 == code.astype(jnp.int32))


def own_facts(given, routes, gates, parents, facts):
    column = flat_iota((1, routes.shape[1]), 1)
    live = (column < given[0]) & (lax.rem(column, given[1]) == given[2])
    scores = gates[...]
    weights = scores / jnp.sum(scores, axis=0, keepdims=True) * jnp.where(live, 1.0, 0.0)
    facts[...] = jnp.zeros_like(facts)
    facts[0:8, :] = jnp.where(live, routes[...], -1).astype(jnp.float32)
    facts[WEIGHT_ROW : WEIGHT_ROW + 8, :] = weights
    facts[PARENT_ROW : PARENT_ROW + 1, :] = parents[...].astype(jnp.float32)


def group_plan(sizes, place, *refs):
    n_rep, n_exp, rows, cap, cap_back, cap_z, cap_z_back = sizes
    blocks = refs[:n_exp]
    facts, pack, unpack, select, expand = refs[n_exp:]
    group = rows * n_exp
    n_pair = n_rep // 2
    my_rep = place[0]
    my_exp = place[1]
    for s in range(n_exp):
        facts[:, s * rows : (s + 1) * rows] = blocks[s][...]
    named = facts[0:8, :]
    parent = facts[PARENT_ROW : PARENT_ROW + 1, :].astype(jnp.int32)
    block = lax.div(parent, rows)
    parent = parent + (lax.rem(my_exp - block + n_exp, n_exp) - block) * rows
    facts[PARENT_ROW : PARENT_ROW + 1, :] = parent.astype(jnp.float32)
    parents = parent_table(parent, group)
    in_block = before_table(group, rows)
    in_group = before_table(group, group)

    lane = named - jnp.floor((named + 0.5) / n_exp) * n_exp
    planes = [any_hit((lane == float(z)) & (named >= 0.0)) for z in range(n_exp)]
    planes = jnp.concatenate(planes + [jnp.zeros_like(planes[0])] * (-n_exp % 8), axis=0)
    wanted = jnp.where(dot_nt(planes.astype(BF16), parents) > 0.5, 1.0, 0.0)
    code_z = code_of(wanted, in_block)
    code_z_back = code_of(planes, in_block)
    for s in range(n_exp):
        plane = lax.rem(my_exp + s, n_exp)
        pack[s * cap_z : (s + 1) * cap_z, :] = slots_of(one_row(code_z[:, :rows], plane), cap_z)
        unpack[s * cap_z_back : (s + 1) * cap_z_back, :] = slots_of(
            one_row(code_z_back[:, :rows], plane), cap_z_back
        )

    turn = lax.div(flat_iota((1, group), 1), rows).astype(jnp.float32)

    def packed(code, slots):
        code = one_row(code, my_exp)
        held = (code > 0.5) & (code < slots + 0.5)
        return slots_of(jnp.where(held, turn * slots + code, 0.0), n_exp * slots)

    held = packed(code_z, cap_z)
    held_back = packed(code_z_back, cap_z_back)

    visits = []
    for pair in range(n_pair):
        for z in range(n_exp):
            first = float(2 * pair * n_exp + z)
            visits.append(any_hit((named == first) | (named == first + n_exp)))
    visits = jnp.concatenate(visits + [jnp.zeros_like(visits[0])] * (-len(visits) % 8), axis=0)
    needs = jnp.where(dot_nt(visits.astype(BF16), parents) > 0.5, 1.0, 0.0)
    code = code_of(needs, in_group)
    code_back = code_of(visits, in_group)
    for k in range(n_pair):
        pair = lax.div(lax.bitwise_xor(my_rep, 2 * k), 2)
        row = pair * n_exp + my_exp
        chosen = slots_of(one_row(code, row), cap)
        select[k * cap : (k + 1) * cap, :] = dot_nt(chosen, held).astype(BF16)
        chosen = slots_of(one_row(code_back, row), cap_back)
        expand[:, k * cap_back : (k + 1) * cap_back] = dot_nt(held_back, chosen).astype(BF16)

    over = jnp.maximum(jnp.max(code_z) - cap_z, jnp.max(code_z_back) - cap_z_back)
    over = jnp.maximum(over, jnp.max(code) - cap)
    over = jnp.maximum(over, jnp.max(code_back) - cap_back)
    facts[FITS_ROW : FITS_ROW + 1, :] = jnp.where(over > 0.5, 0.0, 1.0) * jnp.ones((1, group))


def pair_plan(sizes, place, *refs):
    n_rep, n_exp, rows, cap, cap_back, cap_z, cap_z_back = sizes
    group = rows * n_exp
    n_pair = n_rep // 2
    high, low = refs[n_pair:]
    my_rep = place[0]
    my_exp = place[1]
    in_group = before_table(group, group)
    own = my_rep * n_exp + my_exp
    other = lax.bitwise_xor(my_rep, 1) * n_exp + my_exp
    for k in range(n_pair):
        named = refs[k][0:8, :].astype(jnp.int32)
        weights = refs[k][WEIGHT_ROW : WEIGHT_ROW + 8, :]
        parents = parent_table(refs[k][PARENT_ROW : PARENT_ROW + 1, :], group)
        visit = any_hit((named == own) | (named == other)) * jnp.ones((8, 1), jnp.float32)
        needs = jnp.where(dot_nt(visit.astype(BF16), parents) > 0.5, 1.0, 0.0)
        code = code_of(needs, in_group)[0:1, :]
        code_back = code_of(visit, in_group)[0:1, :]
        source = dot(slots_of(code, cap), parents).astype(BF16)
        target = slots_of(code_back, cap_back).astype(jnp.float32)
        for at, expert in enumerate((own, other)):
            weight = jnp.sum(jnp.where(named == expert, weights, 0.0), axis=0, keepdims=True)
            weight_high = weight.astype(BF16).astype(jnp.float32)
            for out, value in ((high, weight_high), (low, weight - weight_high)):
                table = dot_nt((target * value).astype(BF16), source).astype(BF16)
                out[k * cap_back : (k + 1) * cap_back, at * cap : (at + 1) * cap] = table


def plan_call(body, shapes, place, *tables):
    whole = pl.BlockSpec(memory_space=pltpu.VMEM)
    return pl.pallas_call(
        body,
        out_shape=[jax.ShapeDtypeStruct(shape, kind) for shape, kind in shapes],
        in_specs=[pl.BlockSpec(memory_space=pltpu.SMEM)] + [whole] * len(tables),
        out_specs=[whole] * len(shapes),
        compiler_params=pltpu.CompilerParams(vmem_limit_bytes=48 * 1024 * 1024),
    )(place, *tables)


def column_parts(width, parts):
    unit = width // sum(parts)
    ends = [unit * sum(parts[: i + 1]) for i in range(len(parts))]
    return [slice(end - unit * part, end) for part, end in zip(parts, ends)]


def shards(hidden, parents, routes, gates, counts, norm_gain, w_gate, w_up, w_down):
    rows, width = hidden.shape
    top = routes.shape[1]
    n_rep = lax.axis_size("rep")
    n_exp = lax.axis_size("exp")
    n_pair = n_rep // 2
    group = rows * n_exp
    my_rep = lax.axis_index("rep")
    my_exp = lax.axis_index("exp")
    most = (rows * top // (n_rep * n_exp) + 2) * n_exp
    cap = round_up(most + most // 8, 16)
    cap_back = round_up(most + most // 4, 16)
    cap_z = rows // 2
    cap_z_back = rows // 2
    sizes = (n_rep, n_exp, rows, cap, cap_back, cap_z, cap_z_back)
    place = jnp.stack([my_rep, my_exp]).astype(jnp.int32)

    value = hidden.astype(jnp.float32)
    scale = lax.rsqrt(jnp.mean(value * value, axis=1, keepdims=True) + 1e-06)
    normed = (value * scale * norm_gain).astype(BF16)

    def one_pass(level, index):
        given = jnp.stack([counts[0], level, index])
        (own,) = plan_call(
            own_facts,
            [((FACTS, rows), jnp.float32)],
            given,
            routes.T,
            gates.T,
            parents[None, :],
        )
        blocks = [ring(own, "exp", n_exp, s) for s in range(n_exp)]
        facts, pack, unpack, select, expand = plan_call(
            functools.partial(group_plan, sizes),
            [
                ((FACTS, group), jnp.float32),
                ((n_exp * cap_z, rows), BF16),
                ((n_exp * cap_z_back, rows), BF16),
                ((n_pair * cap, n_exp * cap_z), BF16),
                ((n_exp * cap_z_back, n_pair * cap_back), BF16),
            ],
            place,
            *blocks,
        )
        def packed(cols, normed):
            return [
                dot(pack[s * cap_z : (s + 1) * cap_z], normed[:, cols]).astype(BF16)
                for s in range(n_exp)
            ]

        def along_exp(sent):
            return [ring(sent[s], "exp", n_exp, s) for s in range(n_exp)]

        def to_pairs(held):
            held = jnp.concatenate(held, axis=0)
            sent = [dot(select[k * cap : (k + 1) * cap], held).astype(BF16) for k in range(n_pair)]
            return [flip(sent[k], n_rep, 2 * k) for k in range(n_pair)]

        in_cols = column_parts(width, IN_PARTS)
        last = len(in_cols) - 1
        shared = normed
        sent, facts = lax.optimization_barrier((packed(in_cols[0], shared), facts))
        held = along_exp(sent)
        served = [flip(facts, n_rep, 2 * k) for k in range(n_pair)]
        high, low = plan_call(
            functools.partial(pair_plan, sizes),
            [((n_pair * cap_back, 2 * cap), BF16)] * 2,
            place,
            *served,
        )
        fits = functools.reduce(jnp.minimum, [other[PARENT_ROW:, : 128] for other in served])
        high, shared = lax.optimization_barrier((high, shared))
        ahead = along_exp(packed(in_cols[1], shared))
        moved = to_pairs(held)
        held = ahead
        fits = jnp.minimum(fits, flip(fits, n_rep, 1))
        sums = (0.0, 0.0, 0.0, 0.0)
        for part, cols in enumerate(in_cols):
            if part < last:
                held, shared, sums, high, low, fits = lax.optimization_barrier(
                    (held, shared, sums, high, low, fits)
                )
                after = to_pairs(held)
                if part + 1 < last:
                    held = along_exp(packed(in_cols[part + 2], shared))
            moved, sums = lax.optimization_barrier((moved, sums))
            arrived = jnp.concatenate(moved, axis=0)
            swapped = flip(arrived, n_rep, 1)
            sums = (
                sums[0] + dot(arrived, w_gate[0, cols]),
                sums[1] + dot(arrived, w_up[0, cols]),
                sums[2] + dot(swapped, w_gate[0, cols]),
                sums[3] + dot(swapped, w_up[0, cols]),
            )
            moved = after
        acts = [(jax.nn.silu(sums[i]) * sums[i + 1]).astype(BF16) for i in (0, 2)]

        def weighted(cols, acts):
            given = flip(dot(acts[1], w_down[0, :, cols]).astype(BF16), n_rep, 1)
            own = dot(acts[0], w_down[0, :, cols]).astype(BF16)
            totals = []
            for k in range(n_pair):
                at = slice(k * cap, (k + 1) * cap)
                both = jnp.concatenate([own[at], given[at]], axis=0)
                to = slice(k * cap_back, (k + 1) * cap_back)
                totals.append((dot(high[to], both) + dot(low[to], both)).astype(BF16))
            return totals

        out_cols = column_parts(width, OUT_PARTS)
        last = len(out_cols) - 1
        parts = []
        totals, acts = lax.optimization_barrier((weighted(out_cols[0], acts), acts))
        moved = [flip(totals[k], n_rep, 2 * k) for k in range(n_pair)]
        totals, acts = lax.optimization_barrier((weighted(out_cols[1], acts), acts))
        for part in range(last + 1):
            if part < last:
                after = [flip(totals[k], n_rep, 2 * k) for k in range(n_pair)]
            moved, acts, parts = lax.optimization_barrier((moved, acts, parts))
            partial = dot(expand, jnp.concatenate(moved, axis=0)).astype(BF16)
            parts = parts + [
                [
                    ring(partial[s * cap_z_back : (s + 1) * cap_z_back], "exp", n_exp, -s)
                    for s in range(n_exp)
                ]
            ]
            if part + 1 < last:
                totals = weighted(out_cols[part + 2], acts)
            moved = after
        mixed = [dot_tn(unpack, jnp.concatenate(part, axis=0)).astype(BF16) for part in parts]
        return jnp.concatenate(mixed, axis=1), fits[FITS_ROW - PARENT_ROW, 0] > 0.5

    def unfinished(state):
        return state[1] < state[0]

    def go_on(state):
        level, index, total = state
        mixed, fit = one_pass(level, index)
        total = jnp.where(index == 0, mixed, total + mixed)
        return jnp.where(fit, level, 2 * level), jnp.where(fit, index + 1, 0), total

    start = (jnp.int32(1), jnp.int32(0), jnp.zeros((rows, width), BF16))
    return lax.while_loop(unfinished, go_on, start)[2]


def solution(mesh):
    placed = (
        P(("rep", "exp"), None),
        P(("rep", "exp")),
        P(("rep", "exp"), None),
        P(("rep", "exp"), None),
        P(("rep", "exp")),
        P(),
        P(("rep", "exp"), None, None),
        P(("rep", "exp"), None, None),
        P(("rep", "exp"), None, None),
    )
    return jax.shard_map(
        shards, mesh=mesh, in_specs=placed, out_specs=P(("rep", "exp"), None), check_vma=False
    )
```

profile of v0, /device:TPU:0, one launch (start us, length us, event | category | flops | bytes accessed | tf_op | source)
XLA Modules:
  0.0 228.4 jit_solution(11294739455503727916)
XLA Ops:
  4.3 222.9 %while.12 = (s32[]{:T(128)}, s32[]{:T(128)}, bf16[128,4096]{1,0:T(8,128)(2,1)}, s32[1]{0:T(128)}, s32[128,8]{0,1:T(8,128)S(1)}, /*index=5*/f32[128,8]{0,1:T(8,12...) while((s32[]{:T(128)}, s32[]{:T(128)}, ...), condition=%wide.region_2.3_spmd, body=%wide.region_1.2_spmd.sunk | while | flops 31312318464 | bytes 477694432 | solution.py:348
  6.0 3.1 %collective-permute-start = (f32[24,128]{1,0:T(8,128)S(1)}, f32[24,128]{1,0:T(8,128)S(1)}, u32[]{:S(2)}, u32[]{:S(2)}) collective-permute-start(f32[24,128]{1,0:T(8,128)S(1)} %body.3.refs_0_), channel_id=1, source_target_pairs={{0,1},{1,2},{2,3},{3,0},{4,5},{5,6},{6,7},{7,4},{8,9},{9,10},{10,1... | collective-permute-start | bytes 36872 | tf_op jit(solution)/shard_map/while/body/ppermute | solution.py:38
  9.0 2.6 %collective-permute-start.1 = (f32[24,128]{1,0:T(8,128)S(1)}, f32[24,128]{1,0:T(8,128)S(1)}, u32[]{:S(2)}, u32[]{:S(2)}) collective-permute-start(f32[24,128]{1,0:T(8,128)S(1)} %body.3.refs_0_), channel_id=1, source_target_pairs={{0,2},{1,3},{2,0},{3,1},{4,6},{5,7},{6,4},{7,5},{8,10},{9,11},{10,... | collective-permute-start | bytes 36872 | tf_op jit(solution)/shard_map/while/body/ppermute | solution.py:38
  15.3 2.2 body.4
  21.9 3.6 %collective-permute-start.14 = (bf16[64,1024]{1,0:T(8,128)(2,1)S(1)}, bf16[64,1024]{1,0:T(8,128)(2,1)S(1)}, u32[]{:S(2)}, u32[]{:S(2)}) collective-permute-start(bf16[64,1024]{1,0:T(8,128)(2,1)S(1)} %convolution_convert_fusion.72), channel_id=1, source_target_pairs={{0,2},{1,3},{2,0},{3,1},{4,6},{5,7},{6,4},{7,5},{8,10},{9,11},{10,... | collective-permute-start | bytes 393224 | tf_op jit(solution)/shard_map/while/body/ppermute | solution.py:38
  26.3 4.0 %body.5 = (bf16[704,320]{1,0:T(8,128)(2,1)S(1)}, bf16[704,320]{1,0:T(8,128)(2,1)S(1)}) custom-call(s32[2]{0:T(128)S(1)} %get-tuple-element.613.place, f32[24,512]{1,0:T(8,128)S(1)} %get-tuple-element.439.refs_0_, f32[24,512]{1,0:T(8,128)S(1)} %collective-permute-done.3.refs_1_, f32[24,512]{1,0:T(8,128)S(1)} %collective-permute-done.4.refs_2_, ...), custom_call_target="tpu_custom_call" | custom-call | tf_op jit(solution)/shard_map/while/body/pallas_call | solution.py:192
  31.3 3.2 %collective-permute-start.8 = (bf16[64,1792]{1,0:T(8,128)(2,1)S(1)}, bf16[64,1792]{1,0:T(8,128)(2,1)S(1)}, u32[]{:S(2)}, u32[]{:S(2)}) collective-permute-start(bf16[64,1792]{1,0:T(8,128)(2,1)S(1)} %convolution_convert_fusion.77), channel_id=1, source_target_pairs={{0,3},{1,0},{2,1},{3,2},{4,7},{5,4},{6,5},{7,6},{8,11},{9,8},{10,9... | collective-permute-start | bytes 688136 | tf_op jit(solution)/shard_map/while/body/ppermute | solution.py:38
  41.0 13.8 %collective-permute-done.7 = bf16[64,1792]{1,0:T(8,128)(2,1)S(1)} collective-permute-done((bf16[64,1792]{1,0:T(8,128)(2,1)S(1)}, bf16[64,1792]{1,0:T(8,128)(2,1)S(1)}, u32[]{:S(2)}, u32[]{:S(2)}) %collective-permute-start.7) | collective-permute-done | bytes 229408 | tf_op jit(solution)/shard_map/while/body/ppermute | solution.py:38
  58.2 2.2 collective-permute-start.11
  69.6 2.0 collective-permute-start.10
  72.8 4.1 %collective-permute-done.10 = bf16[64,1280]{1,0:T(8,128)(2,1)S(1)} collective-permute-done((bf16[64,1280]{1,0:T(8,128)(2,1)S(1)}, bf16[64,1280]{1,0:T(8,128)(2,1)S(1)}, u32[]{:S(2)}, u32[]{:S(2)}) %collective-permute-start.10) | collective-permute-done | bytes 163872 | tf_op jit(solution)/shard_map/while/body/ppermute | solution.py:38
  76.9 11.8 %collective-permute-done.24 = bf16[160,1792]{1,0:T(8,128)(2,1)S(1)} collective-permute-done((bf16[160,1792]{1,0:T(8,128)(2,1)S(1)}, bf16[160,1792]{1,0:T(8,128)(2,1)S(1)}, u32[]{:S(2)}, u32[]{:S(2)}) %collective-permute-start.24) | collective-permute-done | bytes 573472 | tf_op jit(solution)/shard_map/while/body/ppermute | solution.py:44
  93.7 2.0 fusion.531
  96.0 2.0 fusion.530
  98.7 1.9 fusion.533
  100.9 2.0 fusion.532
  103.1 7.0 %collective-permute-done.21 = bf16[160,1280]{1,0:T(8,128)(2,1)S(1)} collective-permute-done((bf16[160,1280]{1,0:T(8,128)(2,1)S(1)}, bf16[160,1280]{1,0:T(8,128)(2,1)S(1)}, u32[]{:S(2)}, u32[]{:S(2)}) %collective-permute-start.21) | collective-permute-done | bytes 409632 | tf_op jit(solution)/shard_map/while/body/ppermute | solution.py:44
  113.4 2.0 collective-permute-done.27
  128.5 3.3 %convolution_convert_fusion.96 = bf16[640,1792]{1,0:T(8,128)(2,1)} fusion(bf16[640,768]{1,0:T(8,128)(2,1)S(1)} %multiply_convert_fusion.4, bf16[1,768,4096]{2,1,0:T(8,128)(2,1)S(1)} %bitcast.227), kind=kOutput, calls=%fused_computation.clone.1 | convolution fusion | flops 1762754560 | bytes 6029312 | tf_op jit(solution)/shard_map/while/body/dot_general | solution.py:20
  136.8 4.0 %convolution_convert_fusion.97 = bf16[640,1792]{1,0:T(8,128)(2,1)S(1)} fusion(bf16[640,768]{1,0:T(8,128)(2,1)} %copy-done.4, bf16[1,768,4096]{2,1,0:T(8,128)(2,1)} %get-tuple-element.617), kind=kOutput, calls=%fused_computation.1.clone.1 | convolution fusion | flops 1762754560 | bytes 6029312 | tf_op jit(solution)/shard_map/while/body/dot_general | solution.py:20
  141.0 1.7 fusion.548
  147.0 5.7 %collective-permute-done.31 = bf16[176,1024]{1,0:T(8,128)(2,1)S(1)} collective-permute-done((bf16[176,1024]{1,0:T(8,128)(2,1)S(1)}, bf16[176,1024]{1,0:T(8,128)(2,1)S(1)}, u32[]{:S(2)}, u32[]{:S(2)}) %collective-permute-start.31) | collective-permute-done | bytes 360480 | tf_op jit(solution)/shard_map/while/body/ppermute | solution.py:44
  162.3 1.9 collective-permute-done.41
  165.0 6.0 %collective-permute-done.42 = bf16[64,1024]{1,0:T(8,128)(2,1)S(1)} collective-permute-done((bf16[64,1024]{1,0:T(8,128)(2,1)S(1)}, bf16[64,1024]{1,0:T(8,128)(2,1)S(1)}, u32[]{:S(2)}, u32[]{:S(2)}) %collective-permute-start.42) | collective-permute-done | bytes 131104 | tf_op jit(solution)/shard_map/while/body/ppermute | solution.py:38
  171.0 2.0 collective-permute-done.37
  172.9 11.4 %collective-permute-done.38 = bf16[176,1792]{1,0:T(8,128)(2,1)S(1)} collective-permute-done((bf16[176,1792]{1,0:T(8,128)(2,1)S(1)}, bf16[176,1792]{1,0:T(8,128)(2,1)S(1)}, u32[]{:S(2)}, u32[]{:S(2)}) %collective-permute-start.38) | collective-permute-done | bytes 630816 | tf_op jit(solution)/shard_map/while/body/ppermute | solution.py:44
  185.6 2.1 collective-permute-start.43
  194.4 9.4 %collective-permute-start.45 = (bf16[64,1792]{1,0:T(8,128)(2,1)S(1)}, bf16[64,1792]{1,0:T(8,128)(2,1)S(1)}, u32[]{:S(2)}, u32[]{:S(2)}) collective-permute-start(bf16[64,1792]{1,0:T(8,128)(2,1)S(1)} %get-tuple-element.555), channel_id=1, source_target_pairs={{0,1},{1,2},{2,3},{3,0},{4,5},{5,6},{6,7},{7,4},{8,9},{9,10},{10,1... | collective-permute-start | bytes 688136 | tf_op jit(solution)/shard_map/while/body/ppermute | solution.py:38
  205.6 1.6 collective-permute-done.45
  212.4 2.8 %collective-permute-start.48 = (bf16[64,1280]{1,0:T(8,128)(2,1)S(1)}, bf16[64,1280]{1,0:T(8,128)(2,1)S(1)}, u32[]{:S(2)}, u32[]{:S(2)}) collective-permute-start(bf16[64,1280]{1,0:T(8,128)(2,1)S(1)} %get-tuple-element.562), channel_id=1, source_target_pairs={{0,3},{1,0},{2,1},{3,2},{4,7},{5,4},{6,5},{7,6},{8,11},{9,8},{10,9... | collective-permute-start | bytes 491528 | tf_op jit(solution)/shard_map/while/body/ppermute | solution.py:38
  215.8 2.9 %collective-permute-done.46 = bf16[64,1280]{1,0:T(8,128)(2,1)S(1)} collective-permute-done((bf16[64,1280]{1,0:T(8,128)(2,1)S(1)}, bf16[64,1280]{1,0:T(8,128)(2,1)S(1)}, u32[]{:S(2)}, u32[]{:S(2)}) %collective-permute-start.46) | collective-permute-done | bytes 163872 | tf_op jit(solution)/shard_map/while/body/ppermute | solution.py:38
  218.7 5.9 %collective-permute-done.47 = bf16[64,1280]{1,0:T(8,128)(2,1)S(1)} collective-permute-done((bf16[64,1280]{1,0:T(8,128)(2,1)S(1)}, bf16[64,1280]{1,0:T(8,128)(2,1)S(1)}, u32[]{:S(2)}, u32[]{:S(2)}) %collective-permute-start.47) | collective-permute-done | bytes 163872 | tf_op jit(solution)/shard_map/while/body/ppermute | solution.py:38
  (236 shorter events, 94.2 us)
Async XLA Ops:
  21.8 12.6 %collective-permute-start.13 = (bf16[64,1024]{1,0:T(8,128)(2,1)S(1)}, bf16[64,1024]{1,0:T(8,128)(2,1)S(1)}, u32[]{:S(2)}, u32[]{:S(2)}) collective-permute-start(bf16[64,1024]{1,0:T(8,128)(2,1)S(1)} %convolution_convert_fusion.71), channel_id=1, source_target_pairs={{0,1},{1,2},{2,3},{3,0},{4,5},{5,6},{6,7},{7,4},{8,9},{9,10},{10,1... | collective-permute-start | bytes 393224 | tf_op jit(solution)/shard_map/while/body/ppermute | solution.py:38
  21.9 14.0 %collective-permute-start.14 = (bf16[64,1024]{1,0:T(8,128)(2,1)S(1)}, bf16[64,1024]{1,0:T(8,128)(2,1)S(1)}, u32[]{:S(2)}, u32[]{:S(2)}) collective-permute-start(bf16[64,1024]{1,0:T(8,128)(2,1)S(1)} %convolution_convert_fusion.72), channel_id=1, source_target_pairs={{0,2},{1,3},{2,0},{3,1},{4,6},{5,7},{6,4},{7,5},{8,10},{9,11},{10,... | collective-permute-start | bytes 393224 | tf_op jit(solution)/shard_map/while/body/ppermute | solution.py:38
  25.6 10.4 %collective-permute-start.15 = (bf16[64,1024]{1,0:T(8,128)(2,1)S(1)}, bf16[64,1024]{1,0:T(8,128)(2,1)S(1)}, u32[]{:S(2)}, u32[]{:S(2)}) collective-permute-start(bf16[64,1024]{1,0:T(8,128)(2,1)S(1)} %convolution_convert_fusion.73), channel_id=1, source_target_pairs={{0,3},{1,0},{2,1},{3,2},{4,7},{5,4},{6,5},{7,6},{8,11},{9,8},{10,9... | collective-permute-start | bytes 393224 | tf_op jit(solution)/shard_map/while/body/ppermute | solution.py:38
  34.4 20.3 %collective-permute-start.7 = (bf16[64,1792]{1,0:T(8,128)(2,1)S(1)}, bf16[64,1792]{1,0:T(8,128)(2,1)S(1)}, u32[]{:S(2)}, u32[]{:S(2)}) collective-permute-start(bf16[64,1792]{1,0:T(8,128)(2,1)S(1)} %convolution_convert_fusion.76), channel_id=1, source_target_pairs={{0,2},{1,3},{2,0},{3,1},{4,6},{5,7},{6,4},{7,5},{8,10},{9,11},{10,... | collective-permute-start | bytes 688136 | tf_op jit(solution)/shard_map/while/body/ppermute | solution.py:38
  34.5 20.3 %collective-permute-start.6 = (bf16[64,1792]{1,0:T(8,128)(2,1)S(1)}, bf16[64,1792]{1,0:T(8,128)(2,1)S(1)}, u32[]{:S(2)}, u32[]{:S(2)}) collective-permute-start(bf16[64,1792]{1,0:T(8,128)(2,1)S(1)} %convolution_convert_fusion.75), channel_id=1, source_target_pairs={{0,1},{1,2},{2,3},{3,0},{4,5},{5,6},{6,7},{7,4},{8,9},{9,10},{10,1... | collective-permute-start | bytes 688136 | tf_op jit(solution)/shard_map/while/body/ppermute | solution.py:38
  36.8 19.4 %collective-permute-start.17 = (bf16[160,1024]{1,0:T(8,128)(2,1)S(1)}, bf16[160,1024]{1,0:T(8,128)(2,1)S(1)}, u32[]{:S(2)}, u32[]{:S(2)}) collective-permute-start(bf16[160,1024]{1,0:T(8,128)(2,1)S(1)} %convolution_convert_fusion.84), channel_id=1, source_target_pairs={{0,16},{4,20},{8,24},{12,28},{16,0},{20,4},{24,8},{28,12},{1,17},{... | collective-permute-start | bytes 983048 | tf_op jit(solution)/shard_map/while/body/ppermute | solution.py:44
  37.3 18.8 %collective-permute-start.18 = (bf16[160,1024]{1,0:T(8,128)(2,1)S(1)}, bf16[160,1024]{1,0:T(8,128)(2,1)S(1)}, u32[]{:S(2)}, u32[]{:S(2)}) collective-permute-start(bf16[160,1024]{1,0:T(8,128)(2,1)S(1)} %convolution_convert_fusion.85), channel_id=1, source_target_pairs={{0,24},{4,28},{8,16},{12,20},{16,8},{20,12},{24,0},{28,4},{1,25},{... | collective-permute-start | bytes 983048 | tf_op jit(solution)/shard_map/while/body/ppermute | solution.py:44
  40.4 15.7 %collective-permute-start.16 = (bf16[160,1024]{1,0:T(8,128)(2,1)S(1)}, bf16[160,1024]{1,0:T(8,128)(2,1)S(1)}, u32[]{:S(2)}, u32[]{:S(2)}) collective-permute-start(bf16[160,1024]{1,0:T(8,128)(2,1)S(1)} %convolution_convert_fusion.83), channel_id=1, source_target_pairs={{0,8},{4,12},{8,0},{12,4},{16,24},{20,28},{24,16},{28,20},{1,9},{5... | collective-permute-start | bytes 983048 | tf_op jit(solution)/shard_map/while/body/ppermute | solution.py:44
  56.3 11.7 %collective-permute-start.19 = (bf16[640,1024]{1,0:T(8,128)(2,1)S(1)}, bf16[640,1024]{1,0:T(8,128)(2,1)S(1)}, u32[]{:S(2)}, u32[]{:S(2)}) collective-permute-start(bf16[640,1024]{1,0:T(8,128)(2,1)S(1)} %constant_dynamic-update-slice_fusion.55), channel_id=1, source_target_pairs={{0,4},{4,0},{8,12},{12,8},{16,20},{20,16},{24,28},{28,24},{1,5},{5... | collective-permute-start | bytes 3932168 | tf_op jit(solution)/shard_map/while/body/ppermute | solution.py:44
  56.6 13.0 %collective-permute-start.12 = (bf16[64,1280]{1,0:T(8,128)(2,1)S(1)}, bf16[64,1280]{1,0:T(8,128)(2,1)S(1)}, u32[]{:S(2)}, u32[]{:S(2)}) collective-permute-start(bf16[64,1280]{1,0:T(8,128)(2,1)S(1)} %convolution_convert_fusion.81), channel_id=1, source_target_pairs={{0,3},{1,0},{2,1},{3,2},{4,7},{5,4},{6,5},{7,6},{8,11},{9,8},{10,9... | collective-permute-start | bytes 491528 | tf_op jit(solution)/shard_map/while/body/ppermute | solution.py:38
  58.2 14.7 %collective-permute-start.11 = (bf16[64,1280]{1,0:T(8,128)(2,1)S(1)}, bf16[64,1280]{1,0:T(8,128)(2,1)S(1)}, u32[]{:S(2)}, u32[]{:S(2)}) collective-permute-start(bf16[64,1280]{1,0:T(8,128)(2,1)S(1)} %convolution_convert_fusion.80), channel_id=1, source_target_pairs={{0,2},{1,3},{2,0},{3,1},{4,6},{5,7},{6,4},{7,5},{8,10},{9,11},{10,... | collective-permute-start | bytes 491528 | tf_op jit(solution)/shard_map/while/body/ppermute | solution.py:38
  60.3 16.6 %collective-permute-start.23 = (bf16[160,1792]{1,0:T(8,128)(2,1)S(1)}, bf16[160,1792]{1,0:T(8,128)(2,1)S(1)}, u32[]{:S(2)}, u32[]{:S(2)}) collective-permute-start(bf16[160,1792]{1,0:T(8,128)(2,1)S(1)} %convolution_convert_fusion.91), channel_id=1, source_target_pairs={{0,8},{4,12},{8,0},{12,4},{16,24},{20,28},{24,16},{28,20},{1,9},{5... | collective-permute-start | bytes 1720328 | tf_op jit(solution)/shard_map/while/body/ppermute | solution.py:44
  61.9 26.8 %collective-permute-start.24 = (bf16[160,1792]{1,0:T(8,128)(2,1)S(1)}, bf16[160,1792]{1,0:T(8,128)(2,1)S(1)}, u32[]{:S(2)}, u32[]{:S(2)}) collective-permute-start(bf16[160,1792]{1,0:T(8,128)(2,1)S(1)} %convolution_convert_fusion.92), channel_id=1, source_target_pairs={{0,16},{4,20},{8,24},{12,28},{16,0},{20,4},{24,8},{28,12},{1,17},{... | collective-permute-start | bytes 1720328 | tf_op jit(solution)/shard_map/while/body/ppermute | solution.py:44
  68.0 20.8 %collective-permute-start.25 = (bf16[160,1792]{1,0:T(8,128)(2,1)S(1)}, bf16[160,1792]{1,0:T(8,128)(2,1)S(1)}, u32[]{:S(2)}, u32[]{:S(2)}) collective-permute-start(bf16[160,1792]{1,0:T(8,128)(2,1)S(1)} %convolution_convert_fusion.93), channel_id=1, source_target_pairs={{0,24},{4,28},{8,16},{12,20},{16,8},{20,12},{24,0},{28,4},{1,25},{... | collective-permute-start | bytes 1720328 | tf_op jit(solution)/shard_map/while/body/ppermute | solution.py:44
  89.0 9.7 %collective-permute-start.26 = (bf16[640,1792]{1,0:T(8,128)(2,1)S(1)}, bf16[640,1792]{1,0:T(8,128)(2,1)S(1)}, u32[]{:S(2)}, u32[]{:S(2)}) collective-permute-start(bf16[640,1792]{1,0:T(8,128)(2,1)S(1)} %constant_dynamic-update-slice_fusion.67), channel_id=1, source_target_pairs={{0,4},{4,0},{8,12},{12,8},{16,20},{20,16},{24,28},{28,24},{1,5},{5... | collective-permute-start | bytes 6881288 | tf_op jit(solution)/shard_map/while/body/ppermute | solution.py:44
  89.4 20.7 %collective-permute-start.21 = (bf16[160,1280]{1,0:T(8,128)(2,1)S(1)}, bf16[160,1280]{1,0:T(8,128)(2,1)S(1)}, u32[]{:S(2)}, u32[]{:S(2)}) collective-permute-start(bf16[160,1280]{1,0:T(8,128)(2,1)S(1)} %convolution_convert_fusion.88), channel_id=1, source_target_pairs={{0,16},{4,20},{8,24},{12,28},{16,0},{20,4},{24,8},{28,12},{1,17},{... | collective-permute-start | bytes 1228808 | tf_op jit(solution)/shard_map/while/body/ppermute | solution.py:44
  91.3 18.8 %collective-permute-start.22 = (bf16[160,1280]{1,0:T(8,128)(2,1)S(1)}, bf16[160,1280]{1,0:T(8,128)(2,1)S(1)}, u32[]{:S(2)}, u32[]{:S(2)}) collective-permute-start(bf16[160,1280]{1,0:T(8,128)(2,1)S(1)} %convolution_convert_fusion.89), channel_id=1, source_target_pairs={{0,24},{4,28},{8,16},{12,20},{16,8},{20,12},{24,0},{28,4},{1,25},{... | collective-permute-start | bytes 1228808 | tf_op jit(solution)/shard_map/while/body/ppermute | solution.py:44
  92.8 18.9 %collective-permute-start.20 = (bf16[160,1280]{1,0:T(8,128)(2,1)S(1)}, bf16[160,1280]{1,0:T(8,128)(2,1)S(1)}, u32[]{:S(2)}, u32[]{:S(2)}) collective-permute-start(bf16[160,1280]{1,0:T(8,128)(2,1)S(1)} %convolution_convert_fusion.87), channel_id=1, source_target_pairs={{0,8},{4,12},{8,0},{12,4},{16,24},{20,28},{24,16},{28,20},{1,9},{5... | collective-permute-start | bytes 1228808 | tf_op jit(solution)/shard_map/while/body/ppermute | solution.py:44
  133.3 13.7 %collective-permute-start.29 = (bf16[176,1024]{1,0:T(8,128)(2,1)}, bf16[176,1024]{1,0:T(8,128)(2,1)S(1)}, u32[]{:S(2)}, u32[]{:S(2)}) collective-permute-start(bf16[176,1024]{1,0:T(8,128)(2,1)} %fusion.543), channel_id=1, source_target_pairs={{0,8},{4,12},{8,0},{12,4},{16,24},{20,28},{24,16},{28,20},{1,9},{5... | collective-permute-start | bytes 1081352 | tf_op jit(solution)/shard_map/while/body/ppermute | solution.py:44
  134.6 12.4 %collective-permute-start.30 = (bf16[176,1024]{1,0:T(8,128)(2,1)S(1)}, bf16[176,1024]{1,0:T(8,128)(2,1)S(1)}, u32[]{:S(2)}, u32[]{:S(2)}) collective-permute-start(bf16[176,1024]{1,0:T(8,128)(2,1)S(1)} %fusion.545), channel_id=1, source_target_pairs={{0,16},{4,20},{8,24},{12,28},{16,0},{20,4},{24,8},{28,12},{1,17},{... | collective-permute-start | bytes 1081352 | tf_op jit(solution)/shard_map/while/body/ppermute | solution.py:44
  135.4 17.3 %collective-permute-start.31 = (bf16[176,1024]{1,0:T(8,128)(2,1)S(1)}, bf16[176,1024]{1,0:T(8,128)(2,1)S(1)}, u32[]{:S(2)}, u32[]{:S(2)}) collective-permute-start(bf16[176,1024]{1,0:T(8,128)(2,1)S(1)} %fusion.547), channel_id=1, source_target_pairs={{0,24},{4,28},{8,16},{12,20},{16,8},{20,12},{24,0},{28,4},{1,25},{... | collective-permute-start | bytes 1081352 | tf_op jit(solution)/shard_map/while/body/ppermute | solution.py:44
  155.8 17.1 %collective-permute-start.37 = (bf16[176,1792]{1,0:T(8,128)(2,1)S(1)}, bf16[176,1792]{1,0:T(8,128)(2,1)S(1)}, u32[]{:S(2)}, u32[]{:S(2)}) collective-permute-start(bf16[176,1792]{1,0:T(8,128)(2,1)S(1)} %fusion.553), channel_id=1, source_target_pairs={{0,8},{4,12},{8,0},{12,4},{16,24},{20,28},{24,16},{28,20},{1,9},{5... | collective-permute-start | bytes 1892360 | tf_op jit(solution)/shard_map/while/body/ppermute | solution.py:44
  156.3 28.0 %collective-permute-start.38 = (bf16[176,1792]{1,0:T(8,128)(2,1)S(1)}, bf16[176,1792]{1,0:T(8,128)(2,1)S(1)}, u32[]{:S(2)}, u32[]{:S(2)}) collective-permute-start(bf16[176,1792]{1,0:T(8,128)(2,1)S(1)} %fusion.555), channel_id=1, source_target_pairs={{0,16},{4,20},{8,24},{12,28},{16,0},{20,4},{24,8},{28,12},{1,17},{... | collective-permute-start | bytes 1892360 | tf_op jit(solution)/shard_map/while/body/ppermute | solution.py:44
  157.7 26.6 %collective-permute-start.39 = (bf16[176,1792]{1,0:T(8,128)(2,1)S(1)}, bf16[176,1792]{1,0:T(8,128)(2,1)S(1)}, u32[]{:S(2)}, u32[]{:S(2)}) collective-permute-start(bf16[176,1792]{1,0:T(8,128)(2,1)S(1)} %fusion.557), channel_id=1, source_target_pairs={{0,24},{4,28},{8,16},{12,20},{16,8},{20,12},{24,0},{28,4},{1,25},{... | collective-permute-start | bytes 1892360 | tf_op jit(solution)/shard_map/while/body/ppermute | solution.py:44
  160.8 27.0 %collective-permute-start.33 = (bf16[640,1280]{1,0:T(8,128)(2,1)S(1)}, bf16[640,1280]{1,0:T(8,128)(2,1)S(1)}, u32[]{:S(2)}, u32[]{:S(2)}) collective-permute-start(bf16[640,1280]{1,0:T(8,128)(2,1)S(1)} %convolution_convert_fusion.98), channel_id=1, source_target_pairs={{0,4},{4,0},{8,12},{12,8},{16,20},{20,16},{24,28},{28,24},{1,5},{5... | collective-permute-start | bytes 4915208 | tf_op jit(solution)/shard_map/while/body/ppermute | solution.py:44
  187.8 17.9 %collective-permute-start.44 = (bf16[64,1792]{1,0:T(8,128)(2,1)S(1)}, bf16[64,1792]{1,0:T(8,128)(2,1)S(1)}, u32[]{:S(2)}, u32[]{:S(2)}) collective-permute-start(bf16[64,1792]{1,0:T(8,128)(2,1)S(1)} %get-tuple-element.554), channel_id=1, source_target_pairs={{0,2},{1,3},{2,0},{3,1},{4,6},{5,7},{6,4},{7,5},{8,10},{9,11},{10,... | collective-permute-start | bytes 688136 | tf_op jit(solution)/shard_map/while/body/ppermute | solution.py:38
  188.7 18.6 %collective-permute-start.36 = (bf16[176,1280]{1,0:T(8,128)(2,1)S(1)}, bf16[176,1280]{1,0:T(8,128)(2,1)S(1)}, u32[]{:S(2)}, u32[]{:S(2)}) collective-permute-start(bf16[176,1280]{1,0:T(8,128)(2,1)S(1)} %fusion.567), channel_id=1, source_target_pairs={{0,24},{4,28},{8,16},{12,20},{16,8},{20,12},{24,0},{28,4},{1,25},{... | collective-permute-start | bytes 1351688 | tf_op jit(solution)/shard_map/while/body/ppermute | solution.py:44
  191.0 17.7 %collective-permute-start.35 = (bf16[176,1280]{1,0:T(8,128)(2,1)S(1)}, bf16[176,1280]{1,0:T(8,128)(2,1)S(1)}, u32[]{:S(2)}, u32[]{:S(2)}) collective-permute-start(bf16[176,1280]{1,0:T(8,128)(2,1)S(1)} %fusion.565), channel_id=1, source_target_pairs={{0,16},{4,20},{8,24},{12,28},{16,0},{20,4},{24,8},{28,12},{1,17},{... | collective-permute-start | bytes 1351688 | tf_op jit(solution)/shard_map/while/body/ppermute | solution.py:44
  193.3 15.5 %collective-permute-start.34 = (bf16[176,1280]{1,0:T(8,128)(2,1)S(1)}, bf16[176,1280]{1,0:T(8,128)(2,1)S(1)}, u32[]{:S(2)}, u32[]{:S(2)}) collective-permute-start(bf16[176,1280]{1,0:T(8,128)(2,1)S(1)} %fusion.563), channel_id=1, source_target_pairs={{0,8},{4,12},{8,0},{12,4},{16,24},{20,28},{24,16},{28,20},{1,9},{5... | collective-permute-start | bytes 1351688 | tf_op jit(solution)/shard_map/while/body/ppermute | solution.py:44
  194.4 12.9 %collective-permute-start.45 = (bf16[64,1792]{1,0:T(8,128)(2,1)S(1)}, bf16[64,1792]{1,0:T(8,128)(2,1)S(1)}, u32[]{:S(2)}, u32[]{:S(2)}) collective-permute-start(bf16[64,1792]{1,0:T(8,128)(2,1)S(1)} %get-tuple-element.555), channel_id=1, source_target_pairs={{0,1},{1,2},{2,3},{3,0},{4,5},{5,6},{6,7},{7,4},{8,9},{9,10},{10,1... | collective-permute-start | bytes 688136 | tf_op jit(solution)/shard_map/while/body/ppermute | solution.py:38
  211.2 13.4 %collective-permute-start.47 = (bf16[64,1280]{1,0:T(8,128)(2,1)S(1)}, bf16[64,1280]{1,0:T(8,128)(2,1)S(1)}, u32[]{:S(2)}, u32[]{:S(2)}) collective-permute-start(bf16[64,1280]{1,0:T(8,128)(2,1)S(1)} %get-tuple-element.561), channel_id=1, source_target_pairs={{0,2},{1,3},{2,0},{3,1},{4,6},{5,7},{6,4},{7,5},{8,10},{9,11},{10,... | collective-permute-start | bytes 491528 | tf_op jit(solution)/shard_map/while/body/ppermute | solution.py:38
  212.4 12.2 %collective-permute-start.48 = (bf16[64,1280]{1,0:T(8,128)(2,1)S(1)}, bf16[64,1280]{1,0:T(8,128)(2,1)S(1)}, u32[]{:S(2)}, u32[]{:S(2)}) collective-permute-start(bf16[64,1280]{1,0:T(8,128)(2,1)S(1)} %get-tuple-element.562), channel_id=1, source_target_pairs={{0,3},{1,0},{2,1},{3,2},{4,7},{5,4},{6,5},{7,6},{8,11},{9,8},{10,9... | collective-permute-start | bytes 491528 | tf_op jit(solution)/shard_map/while/body/ppermute | solution.py:38
  (37 other events, 242.3 us)
where the time goes:
time: 231 us; the launch traced here: 228 us
  waiting for transfers between devices  85.2 us (37%)
  starting transfers between devices  66.6 us (29%)
  matrix products  51.8 us (22%)
  local copies, waits for them, and re-layouts  7.04 us (3%)
  other arithmetic  6.93 us (3%)
  Pallas kernels  6.83 us (3%)
  loops' own time  2.84 us (1%)
    dot_general x69, matrix products, dot(): return jnp.dot(a, b, preferred_element_type=jnp.float32)  51 us
    ppermute x28, waiting for transfers between devices, flip(): return lax.ppermute(value, 'rep', [(i, i ^ mask) for i in range(size)])  43.7 us
    ppermute x21, starting transfers between devices, ring(): lax.ppermute(value, axis, [(i, (i + shift) % size) for i in range(size)])  41.5 us
    ppermute x21, waiting for transfers between devices, ring(): lax.ppermute(value, axis, [(i, (i + shift) % size) for i in range(size)])  41.4 us
    ppermute x28, starting transfers between devices, flip(): return lax.ppermute(value, 'rep', [(i, i ^ mask) for i in range(size)])  25.1 us
    pallas_call x3, Pallas kernels, plan_call(): pl.pallas_call(body, out_shape=[jax.ShapeDtypeStruct(shape, kind) for sha...  6.83 us
  transfers between devices with their start and end apart: 49, of which 21 were waited for; matrix products, arithmetic and copies ran while one was open for 19% of the time, Pallas kernels for 2%

commit v1 on v0

--- a/solution.py
+++ b/solution.py
@@ -184,7 +184,7 @@
             weight_high = weight.astype(BF16).astype(jnp.float32)
             for out, value in ((high, weight_high), (low, weight - weight_high)):
                 table = dot_nt((target * value).astype(BF16), source).astype(BF16)
-                out[k * cap_back : (k + 1) * cap_back, at * cap : (at + 1) * cap] = table
+                out[k, :, at * cap : (at + 1) * cap] = table
 
 
 def plan_call(body, shapes, place, *tables):
@@ -221,10 +221,6 @@
     sizes = (n_rep, n_exp, rows, cap, cap_back, cap_z, cap_z_back)
     place = jnp.stack([my_rep, my_exp]).astype(jnp.int32)
 
-    value = hidden.astype(jnp.float32)
-    scale = lax.rsqrt(jnp.mean(value * value, axis=1, keepdims=True) + 1e-06)
-    normed = (value * scale * norm_gain).astype(BF16)
-
     def one_pass(level, index):
         given = jnp.stack([counts[0], level, index])
         (own,) = plan_call(
@@ -235,7 +231,11 @@
             gates.T,
             parents[None, :],
         )
+        own, rows_in = lax.optimization_barrier((own, hidden))
         blocks = [ring(own, "exp", n_exp, s) for s in range(n_exp)]
+        value = rows_in.astype(jnp.float32)
+        scale = lax.rsqrt(jnp.mean(value * value, axis=1, keepdims=True) + 1e-06)
+        normed = (value * scale * norm_gain).astype(BF16)
         facts, pack, unpack, select, expand = plan_call(
             functools.partial(group_plan, sizes),
             [
@@ -270,7 +270,7 @@
         served = [flip(facts, n_rep, 2 * k) for k in range(n_pair)]
         high, low = plan_call(
             functools.partial(pair_plan, sizes),
-            [((n_pair * cap_back, 2 * cap), BF16)] * 2,
+            [((n_pair, cap_back, 2 * cap), BF16)] * 2,
             place,
             *served,
         )
@@ -304,12 +304,12 @@
         def weighted(cols, acts):
             given = flip(dot(acts[1], w_down[0, :, cols]).astype(BF16), n_rep, 1)
             own = dot(acts[0], w_down[0, :, cols]).astype(BF16)
-            totals = []
-            for k in range(n_pair):
-                at = slice(k * cap, (k + 1) * cap)
-                both = jnp.concatenate([own[at], given[at]], axis=0)
-                to = slice(k * cap_back, (k + 1) * cap_back)
-                totals.append((dot(high[to], both) + dot(low[to], both)).astype(BF16))
+            both = jnp.concatenate(
+                [own.reshape(n_pair, cap, -1), given.reshape(n_pair, cap, -1)], axis=1
+            )
+            total = jnp.einsum("krs,ksd->krd", high, both, preferred_element_type=jnp.float32)
+            total += jnp.einsum("krs,ksd->krd", low, both, preferred_element_type=jnp.float32)
+            totals = total.astype(BF16)
             return totals
 
         out_cols = column_parts(width, OUT_PARTS)
@@ -319,9 +319,9 @@
         moved = [flip(totals[k], n_rep, 2 * k) for k in range(n_pair)]
         totals, acts = lax.optimization_barrier((weighted(out_cols[1], acts), acts))
         for part in range(last + 1):
+            moved, totals, acts, parts = lax.optimization_barrier((moved, totals, acts, parts))
             if part < last:
                 after = [flip(totals[k], n_rep, 2 * k) for k in range(n_pair)]
-            moved, acts, parts = lax.optimization_barrier((moved, acts, parts))
             partial = dot(expand, jnp.concatenate(moved, axis=0)).astype(BF16)
             parts = parts + [
                 [

time: 231 us -> 227 us (0.983)
  starting transfers between devices: 66.6 us -> 55.1 us
  waiting for transfers between devices: 85.2 us -> 93.5 us
    ppermute x21, starting transfers between devices: 41.5 us -> 29.4 us  [ring(): lax.ppermute(value, axis, [(i, (i + shift) % size) for i in range(size)])]
    dot_general x0 -> x6, matrix products: none -> 7.79 us  [the longest x3 4.31 us: weighted(): jnp.einsum('krs,ksd->krd', high, both, preferred_element_type=jnp.float32)]
    dot_general x69 -> x45, matrix products: 51 us -> 43.3 us  [dot(): return jnp.dot(a, b, preferred_element_type=jnp.float32)]
    ppermute x21, waiting for transfers between devices: 41.4 us -> 48.2 us  [ring(): lax.ppermute(value, axis, [(i, (i + shift) % size) for i in range(size)])]
    slice x6 -> x0, local copies, waits for them, and re-layouts: 2.36 us -> none  [weighted(): both = jnp.concatenate([own[at], given[at]], axis=0)]
  transfers between devices with their start and end apart: 49 -> 49, of which waited for: 21 -> 20; matrix products, arithmetic and copies ran while one was open for 19% -> 19% of each run, Pallas kernels for 2% -> 2%
where the time goes in v1:
time: 227 us; the launch traced here: 225 us
  waiting for transfers between devices  93.5 us (41%)
  starting transfers between devices  55.1 us (24%)
  matrix products  53 us (23%)
  other arithmetic  7.17 us (3%)
  Pallas kernels  6.99 us (3%)
  local copies, waits for them, and re-layouts  6.23 us (3%)
  loops' own time  3.13 us (1%)
    ppermute x21, waiting for transfers between devices, ring(): lax.ppermute(value, axis, [(i, (i + shift) % size) for i in range(size)])  48.2 us
    ppermute x28, waiting for transfers between devices, flip(): return lax.ppermute(value, 'rep', [(i, i ^ mask) for i in range(size)])  45.2 us
    dot_general x45, matrix products, dot(): return jnp.dot(a, b, preferred_element_type=jnp.float32)  43.3 us
    ppermute x21, starting transfers between devices, ring(): lax.ppermute(value, axis, [(i, (i + shift) % size) for i in range(size)])  29.4 us
    ppermute x28, starting transfers between devices, flip(): return lax.ppermute(value, 'rep', [(i, i ^ mask) for i in range(size)])  25.7 us
    pallas_call x3, Pallas kernels, plan_call(): pl.pallas_call(body, out_shape=[jax.ShapeDtypeStruct(shape, kind) for sha...  6.99 us
  transfers between devices with their start and end apart: 49, of which 20 were waited for; matrix products, arithmetic and copies ran while one was open for 19% of the time, Pallas kernels for 2%

profile of v1, /device:TPU:0, one launch (start us, length us, event | category | flops | bytes accessed | tf_op | source)
XLA Modules:
  0.0 225.4 jit_solution(1147180609276914794)
XLA Ops:
  0.2 224.0 %while.12 = (s32[]{:T(128)}, s32[]{:T(128)}, bf16[128,4096]{1,0:T(8,128)(2,1)S(1)}, s32[1]{0:T(128)}, s32[128,8]{0,1:T(8,128)}, /*index=5*/f32[128,8]{0,1:T(8,12...) while((s32[]{:T(128)}, s32[]{:T(128)}, ...), condition=%wide.region_2.3_spmd, body=%wide.region_0.2_spmd.sunk | while | flops 31315988480 | bytes 413077952 | solution.py:348
  2.2 3.1 %collective-permute-start = (f32[24,128]{1,0:T(8,128)S(1)}, f32[24,128]{1,0:T(8,128)S(1)}, u32[]{:S(2)}, u32[]{:S(2)}) collective-permute-start(f32[24,128]{1,0:T(8,128)S(1)} %body.3.refs_0_), channel_id=1, source_target_pairs={{0,1},{1,2},{2,3},{3,0},{4,5},{5,6},{6,7},{7,4},{8,9},{9,10},{10,1... | collective-permute-start | bytes 36872 | tf_op jit(solution)/shard_map/while/body/ppermute | solution.py:38
  5.3 2.6 %collective-permute-start.1 = (f32[24,128]{1,0:T(8,128)S(1)}, f32[24,128]{1,0:T(8,128)S(1)}, u32[]{:S(2)}, u32[]{:S(2)}) collective-permute-start(f32[24,128]{1,0:T(8,128)S(1)} %body.3.refs_0_), channel_id=1, source_target_pairs={{0,2},{1,3},{2,0},{3,1},{4,6},{5,7},{6,4},{7,5},{8,10},{9,11},{10,... | collective-permute-start | bytes 36872 | tf_op jit(solution)/shard_map/while/body/ppermute | solution.py:38
  12.3 2.2 body.4
  19.6 2.3 %collective-permute-start.14 = (bf16[64,1024]{1,0:T(8,128)(2,1)S(1)}, bf16[64,1024]{1,0:T(8,128)(2,1)S(1)}, u32[]{:S(2)}, u32[]{:S(2)}) collective-permute-start(bf16[64,1024]{1,0:T(8,128)(2,1)S(1)} %convolution_convert_fusion.72), channel_id=1, source_target_pairs={{0,2},{1,3},{2,0},{3,1},{4,6},{5,7},{6,4},{7,5},{8,10},{9,11},{10,... | collective-permute-start | bytes 393224 | tf_op jit(solution)/shard_map/while/body/ppermute | solution.py:38
  23.3 4.0 %body.5 = (bf16[4,176,320]{2,1,0:T(8,128)(2,1)S(1)}, bf16[4,176,320]{2,1,0:T(8,128)(2,1)S(1)}) custom-call(s32[2]{0:T(128)S(1)} %get-tuple-element.587.place, f32[24,512]{1,0:T(8,128)S(1)} %get-tuple-element.426.refs_0_, f32[24,512]{1,0:T(8,128)S(1)} %collective-permute-done.3.refs_1_, f32[24,512]{1,0:T(8,128)S(1)} %collective-permute-done.4.refs_2_, ...), custom_call_target="tpu_custom_call" | custom-call | tf_op jit(solution)/shard_map/while/body/pallas_call | solution.py:192
  28.3 2.4 %collective-permute-start.8 = (bf16[64,1792]{1,0:T(8,128)(2,1)S(1)}, bf16[64,1792]{1,0:T(8,128)(2,1)S(1)}, u32[]{:S(2)}, u32[]{:S(2)}) collective-permute-start(bf16[64,1792]{1,0:T(8,128)(2,1)S(1)} %convolution_convert_fusion.77), channel_id=1, source_target_pairs={{0,3},{1,0},{2,1},{3,2},{4,7},{5,4},{6,5},{7,6},{8,11},{9,8},{10,9... | collective-permute-start | bytes 688136 | tf_op jit(solution)/shard_map/while/body/ppermute | solution.py:38
  33.0 2.1 collective-permute-start.18
  37.2 14.6 %collective-permute-done.7 = bf16[64,1792]{1,0:T(8,128)(2,1)S(1)} collective-permute-done((bf16[64,1792]{1,0:T(8,128)(2,1)S(1)}, bf16[64,1792]{1,0:T(8,128)(2,1)S(1)}, u32[]{:S(2)}, u32[]{:S(2)}) %collective-permute-start.7) | collective-permute-done | bytes 229408 | tf_op jit(solution)/shard_map/while/body/ppermute | solution.py:38
  61.9 3.3 %collective-permute-start.11 = (bf16[64,1280]{1,0:T(8,128)(2,1)S(1)}, bf16[64,1280]{1,0:T(8,128)(2,1)S(1)}, u32[]{:S(2)}, u32[]{:S(2)}) collective-permute-start(bf16[64,1280]{1,0:T(8,128)(2,1)S(1)} %convolution_convert_fusion.80), channel_id=1, source_target_pairs={{0,2},{1,3},{2,0},{3,1},{4,6},{5,7},{6,4},{7,5},{8,10},{9,11},{10,... | collective-permute-start | bytes 491528 | tf_op jit(solution)/shard_map/while/body/ppermute | solution.py:38
  68.6 7.3 %collective-permute-done.11 = bf16[64,1280]{1,0:T(8,128)(2,1)S(1)} collective-permute-done((bf16[64,1280]{1,0:T(8,128)(2,1)S(1)}, bf16[64,1280]{1,0:T(8,128)(2,1)S(1)}, u32[]{:S(2)}, u32[]{:S(2)}) %collective-permute-start.11) | collective-permute-done | bytes 163872 | tf_op jit(solution)/shard_map/while/body/ppermute | solution.py:38
  75.9 6.8 %collective-permute-done.24 = bf16[160,1792]{1,0:T(8,128)(2,1)S(1)} collective-permute-done((bf16[160,1792]{1,0:T(8,128)(2,1)S(1)}, bf16[160,1792]{1,0:T(8,128)(2,1)S(1)}, u32[]{:S(2)}, u32[]{:S(2)}) %collective-permute-start.24) | collective-permute-done | bytes 573472 | tf_op jit(solution)/shard_map/while/body/ppermute | solution.py:44
  97.2 6.8 %collective-permute-done.21 = bf16[160,1280]{1,0:T(8,128)(2,1)S(1)} collective-permute-done((bf16[160,1280]{1,0:T(8,128)(2,1)S(1)}, bf16[160,1280]{1,0:T(8,128)(2,1)S(1)}, u32[]{:S(2)}, u32[]{:S(2)}) %collective-permute-start.21) | collective-permute-done | bytes 409632 | tf_op jit(solution)/shard_map/while/body/ppermute | solution.py:44
  105.9 3.0 %fusion.416 = f32[640,768]{1,0:T(8,128)S(1)} fusion(bf16[640,1280]{1,0:T(8,128)(2,1)S(1)} %constant_dynamic-update-slice_fusion.71, bf16[1,4096,768]{2,1,0:T(8,128)(2,1)} %get-tuple-element.590), kind=kOutput, calls=%fused_computation.65.clone.1 | convolution fusion | flops 1258291200 | bytes 5570560 | tf_op jit(solution)/shard_map/while/body/dot_general | solution.py:20
  109.3 3.0 %fusion.414 = f32[640,768]{1,0:T(8,128)S(1)} fusion(bf16[640,1280]{1,0:T(8,128)(2,1)S(1)} %collective-permute-done.27, bf16[1,4096,768]{2,1,0:T(8,128)(2,1)} %get-tuple-element.590), kind=kOutput, calls=%fused_computation.63.clone.1 | convolution fusion | flops 1258291200 | bytes 5570560 | tf_op jit(solution)/shard_map/while/body/dot_general | solution.py:20
  114.6 2.6 %convolution_convert_fusion.94 = bf16[640,1024]{1,0:T(8,128)(2,1)S(1)} fusion(bf16[640,768]{1,0:T(8,128)(2,1)S(1)} %multiply_convert_fusion.4, bf16[1,768,4096]{2,1,0:T(8,128)(2,1)} %get-tuple-element.591), kind=kOutput, calls=%fused_computation.87.clone.1 | convolution fusion | flops 1007288320 | bytes 3866624 | tf_op jit(solution)/shard_map/while/body/dot_general | solution.py:20
  119.5 2.7 %convolution_convert_fusion.95 = bf16[640,1024]{1,0:T(8,128)(2,1)S(1)} fusion(bf16[640,768]{1,0:T(8,128)(2,1)S(1)} %multiply_convert_fusion.5, bf16[1,768,4096]{2,1,0:T(8,128)(2,1)} %get-tuple-element.591), kind=kOutput, calls=%fused_computation.88.clone.1 | convolution fusion | flops 1007288320 | bytes 3866624 | tf_op jit(solution)/shard_map/while/body/dot_general | solution.py:20
  124.1 2.0 convolution_convert_fusion.96
  130.2 2.0 convolution_convert_fusion.97
  133.7 2.3 %add_convert_fusion.5 = bf16[4,176,1792]{2,1,0:T(8,128)(2,1)S(1)} fusion(f32[4,176,1792]{2,1,0:T(8,128)S(1)} %fusion.419, bf16[4,176,320]{2,1,0:T(8,128)(2,1)S(1)} %get-tuple-element.484, bf16[4,160,1792]{2,1,0:T(8,128)(2,1)S(1)} %bitcast.288, bf16[4,160,1792]{2,1,0:T(8,128)(2,1)S(1)} %bitcast.290), kind=kOutput, calls=%fused_computation.clone.1 | convolution fusion | flops 819101696 | bytes 12607488 | tf_op jit(solution)/shard_map/while/body/krs,ksd->krd/dot_general | solution.py:310
  136.0 2.0 collective-permute-done.29
  138.0 6.2 %collective-permute-done.30 = bf16[176,1024]{1,0:T(8,128)(2,1)S(1)} collective-permute-done((bf16[176,1024]{1,0:T(8,128)(2,1)S(1)}, bf16[176,1024]{1,0:T(8,128)(2,1)S(1)}, u32[]{:S(2)}, u32[]{:S(2)}) %collective-permute-start.30) | collective-permute-done | bytes 360480 | tf_op jit(solution)/shard_map/while/body/ppermute | solution.py:44
  148.7 3.3 %collective-permute-start.38 = (bf16[64,1024]{1,0:T(8,128)(2,1)S(1)}, bf16[64,1024]{1,0:T(8,128)(2,1)S(1)}, u32[]{:S(2)}, u32[]{:S(2)}) collective-permute-start(bf16[64,1024]{1,0:T(8,128)(2,1)S(1)} %get-tuple-element.508), channel_id=1, source_target_pairs={{0,2},{1,3},{2,0},{3,1},{4,6},{5,7},{6,4},{7,5},{8,10},{9,11},{10,... | collective-permute-start | bytes 393224 | tf_op jit(solution)/shard_map/while/body/ppermute | solution.py:38
  161.5 3.7 %collective-permute-done.39 = bf16[64,1024]{1,0:T(8,128)(2,1)S(1)} collective-permute-done((bf16[64,1024]{1,0:T(8,128)(2,1)S(1)}, bf16[64,1024]{1,0:T(8,128)(2,1)S(1)}, u32[]{:S(2)}, u32[]{:S(2)}) %collective-permute-start.39) | collective-permute-done | bytes 131104 | tf_op jit(solution)/shard_map/while/body/ppermute | solution.py:38
  165.2 4.1 %collective-permute-done.33 = bf16[176,1792]{1,0:T(8,128)(2,1)S(1)} collective-permute-done((bf16[176,1792]{1,0:T(8,128)(2,1)S(1)}, bf16[176,1792]{1,0:T(8,128)(2,1)S(1)}, u32[]{:S(2)}, u32[]{:S(2)}) %collective-permute-start.33) | collective-permute-done | bytes 630816 | tf_op jit(solution)/shard_map/while/body/ppermute | solution.py:44
  169.3 13.0 %collective-permute-done.34 = bf16[176,1792]{1,0:T(8,128)(2,1)S(1)} collective-permute-done((bf16[176,1792]{1,0:T(8,128)(2,1)S(1)}, bf16[176,1792]{1,0:T(8,128)(2,1)S(1)}, u32[]{:S(2)}, u32[]{:S(2)}) %collective-permute-start.34) | collective-permute-done | bytes 630816 | tf_op jit(solution)/shard_map/while/body/ppermute | solution.py:44
  193.3 12.4 %collective-permute-done.44 = bf16[64,1792]{1,0:T(8,128)(2,1)} collective-permute-done((bf16[64,1792]{1,0:T(8,128)(2,1)}, bf16[64,1792]{1,0:T(8,128)(2,1)}, u32[]{:S(2)}, u32[]{:S(2)}) %collective-permute-start.44) | collective-permute-done | bytes 229408 | tf_op jit(solution)/shard_map/while/body/ppermute | solution.py:38
  205.6 2.0 collective-permute-done.41
  207.6 2.0 convolution_convert_fusion.101
  211.1 2.5 %collective-permute-start.48 = (bf16[64,1280]{1,0:T(8,128)(2,1)S(1)}, bf16[64,1280]{1,0:T(8,128)(2,1)S(1)}, u32[]{:S(2)}, u32[]{:S(2)}) collective-permute-start(bf16[64,1280]{1,0:T(8,128)(2,1)S(1)} %get-tuple-element.533), channel_id=1, source_target_pairs={{0,3},{1,0},{2,1},{3,2},{4,7},{5,4},{6,5},{7,6},{8,11},{9,8},{10,9... | collective-permute-start | bytes 491528 | tf_op jit(solution)/shard_map/while/body/ppermute | solution.py:38
  215.3 3.5 %collective-permute-done.46 = bf16[64,1280]{1,0:T(8,128)(2,1)S(1)} collective-permute-done((bf16[64,1280]{1,0:T(8,128)(2,1)S(1)}, bf16[64,1280]{1,0:T(8,128)(2,1)S(1)}, u32[]{:S(2)}, u32[]{:S(2)}) %collective-permute-start.46) | collective-permute-done | bytes 163872 | tf_op jit(solution)/shard_map/while/body/ppermute | solution.py:38
  218.7 3.6 %collective-permute-done.47 = bf16[64,1280]{1,0:T(8,128)(2,1)S(1)} collective-permute-done((bf16[64,1280]{1,0:T(8,128)(2,1)S(1)}, bf16[64,1280]{1,0:T(8,128)(2,1)S(1)}, u32[]{:S(2)}, u32[]{:S(2)}) %collective-permute-start.47) | collective-permute-done | bytes 163872 | tf_op jit(solution)/shard_map/while/body/ppermute | solution.py:38
  (205 shorter events, 88.7 us)
Async XLA Ops:
  2.2 10.1 %collective-permute-start = (f32[24,128]{1,0:T(8,128)S(1)}, f32[24,128]{1,0:T(8,128)S(1)}, u32[]{:S(2)}, u32[]{:S(2)}) collective-permute-start(f32[24,128]{1,0:T(8,128)S(1)} %body.3.refs_0_), channel_id=1, source_target_pairs={{0,1},{1,2},{2,3},{3,0},{4,5},{5,6},{6,7},{7,4},{8,9},{9,10},{10,1... | collective-permute-start | bytes 36872 | tf_op jit(solution)/shard_map/while/body/ppermute | solution.py:38
  18.8 11.9 %collective-permute-start.13 = (bf16[64,1024]{1,0:T(8,128)(2,1)S(1)}, bf16[64,1024]{1,0:T(8,128)(2,1)S(1)}, u32[]{:S(2)}, u32[]{:S(2)}) collective-permute-start(bf16[64,1024]{1,0:T(8,128)(2,1)S(1)} %convolution_convert_fusion.71), channel_id=1, source_target_pairs={{0,1},{1,2},{2,3},{3,0},{4,5},{5,6},{6,7},{7,4},{8,9},{9,10},{10,1... | collective-permute-start | bytes 393224 | tf_op jit(solution)/shard_map/while/body/ppermute | solution.py:38
  19.6 12.6 %collective-permute-start.14 = (bf16[64,1024]{1,0:T(8,128)(2,1)S(1)}, bf16[64,1024]{1,0:T(8,128)(2,1)S(1)}, u32[]{:S(2)}, u32[]{:S(2)}) collective-permute-start(bf16[64,1024]{1,0:T(8,128)(2,1)S(1)} %convolution_convert_fusion.72), channel_id=1, source_target_pairs={{0,2},{1,3},{2,0},{3,1},{4,6},{5,7},{6,4},{7,5},{8,10},{9,11},{10,... | collective-permute-start | bytes 393224 | tf_op jit(solution)/shard_map/while/body/ppermute | solution.py:38
  21.8 10.4 %collective-permute-start.15 = (bf16[64,1024]{1,0:T(8,128)(2,1)S(1)}, bf16[64,1024]{1,0:T(8,128)(2,1)S(1)}, u32[]{:S(2)}, u32[]{:S(2)}) collective-permute-start(bf16[64,1024]{1,0:T(8,128)(2,1)S(1)} %convolution_convert_fusion.73), channel_id=1, source_target_pairs={{0,3},{1,0},{2,1},{3,2},{4,7},{5,4},{6,5},{7,6},{8,11},{9,8},{10,9... | collective-permute-start | bytes 393224 | tf_op jit(solution)/shard_map/while/body/ppermute | solution.py:38
  30.7 21.2 %collective-permute-start.7 = (bf16[64,1792]{1,0:T(8,128)(2,1)S(1)}, bf16[64,1792]{1,0:T(8,128)(2,1)S(1)}, u32[]{:S(2)}, u32[]{:S(2)}) collective-permute-start(bf16[64,1792]{1,0:T(8,128)(2,1)S(1)} %convolution_convert_fusion.76), channel_id=1, source_target_pairs={{0,2},{1,3},{2,0},{3,1},{4,6},{5,7},{6,4},{7,5},{8,10},{9,11},{10,... | collective-permute-start | bytes 688136 | tf_op jit(solution)/shard_map/while/body/ppermute | solution.py:38
  30.7 21.1 %collective-permute-start.6 = (bf16[64,1792]{1,0:T(8,128)(2,1)S(1)}, bf16[64,1792]{1,0:T(8,128)(2,1)S(1)}, u32[]{:S(2)}, u32[]{:S(2)}) collective-permute-start(bf16[64,1792]{1,0:T(8,128)(2,1)S(1)} %convolution_convert_fusion.75), channel_id=1, source_target_pairs={{0,1},{1,2},{2,3},{3,0},{4,5},{5,6},{6,7},{7,4},{8,9},{9,10},{10,1... | collective-permute-start | bytes 688136 | tf_op jit(solution)/shard_map/while/body/ppermute | solution.py:38
  33.0 20.3 %collective-permute-start.18 = (bf16[160,1024]{1,0:T(8,128)(2,1)S(1)}, bf16[160,1024]{1,0:T(8,128)(2,1)S(1)}, u32[]{:S(2)}, u32[]{:S(2)}) collective-permute-start(bf16[160,1024]{1,0:T(8,128)(2,1)S(1)} %convolution_convert_fusion.85), channel_id=1, source_target_pairs={{0,24},{4,28},{8,16},{12,20},{16,8},{20,12},{24,0},{28,4},{1,25},{... | collective-permute-start | bytes 983048 | tf_op jit(solution)/shard_map/while/body/ppermute | solution.py:44
  35.1 18.2 %collective-permute-start.17 = (bf16[160,1024]{1,0:T(8,128)(2,1)S(1)}, bf16[160,1024]{1,0:T(8,128)(2,1)S(1)}, u32[]{:S(2)}, u32[]{:S(2)}) collective-permute-start(bf16[160,1024]{1,0:T(8,128)(2,1)S(1)} %convolution_convert_fusion.84), channel_id=1, source_target_pairs={{0,16},{4,20},{8,24},{12,28},{16,0},{20,4},{24,8},{28,12},{1,17},{... | collective-permute-start | bytes 983048 | tf_op jit(solution)/shard_map/while/body/ppermute | solution.py:44
  36.7 16.7 %collective-permute-start.16 = (bf16[160,1024]{1,0:T(8,128)(2,1)S(1)}, bf16[160,1024]{1,0:T(8,128)(2,1)S(1)}, u32[]{:S(2)}, u32[]{:S(2)}) collective-permute-start(bf16[160,1024]{1,0:T(8,128)(2,1)S(1)} %convolution_convert_fusion.83), channel_id=1, source_target_pairs={{0,8},{4,12},{8,0},{12,4},{16,24},{20,28},{24,16},{28,20},{1,9},{5... | collective-permute-start | bytes 983048 | tf_op jit(solution)/shard_map/while/body/ppermute | solution.py:44
  53.8 22.2 %collective-permute-start.23 = (bf16[160,1792]{1,0:T(8,128)(2,1)S(1)}, bf16[160,1792]{1,0:T(8,128)(2,1)S(1)}, u32[]{:S(2)}, u32[]{:S(2)}) collective-permute-start(bf16[160,1792]{1,0:T(8,128)(2,1)S(1)} %convolution_convert_fusion.91), channel_id=1, source_target_pairs={{0,8},{4,12},{8,0},{12,4},{16,24},{20,28},{24,16},{28,20},{1,9},{5... | collective-permute-start | bytes 1720328 | tf_op jit(solution)/shard_map/while/body/ppermute | solution.py:44
  55.3 27.4 %collective-permute-start.24 = (bf16[160,1792]{1,0:T(8,128)(2,1)S(1)}, bf16[160,1792]{1,0:T(8,128)(2,1)S(1)}, u32[]{:S(2)}, u32[]{:S(2)}) collective-permute-start(bf16[160,1792]{1,0:T(8,128)(2,1)S(1)} %convolution_convert_fusion.92), channel_id=1, source_target_pairs={{0,16},{4,20},{8,24},{12,28},{16,0},{20,4},{24,8},{28,12},{1,17},{... | collective-permute-start | bytes 1720328 | tf_op jit(solution)/shard_map/while/body/ppermute | solution.py:44
  56.9 25.9 %collective-permute-start.25 = (bf16[160,1792]{1,0:T(8,128)(2,1)S(1)}, bf16[160,1792]{1,0:T(8,128)(2,1)S(1)}, u32[]{:S(2)}, u32[]{:S(2)}) collective-permute-start(bf16[160,1792]{1,0:T(8,128)(2,1)S(1)} %convolution_convert_fusion.93), channel_id=1, source_target_pairs={{0,24},{4,28},{8,16},{12,20},{16,8},{20,12},{24,0},{28,4},{1,25},{... | collective-permute-start | bytes 1720328 | tf_op jit(solution)/shard_map/while/body/ppermute | solution.py:44
  61.9 14.1 %collective-permute-start.11 = (bf16[64,1280]{1,0:T(8,128)(2,1)S(1)}, bf16[64,1280]{1,0:T(8,128)(2,1)S(1)}, u32[]{:S(2)}, u32[]{:S(2)}) collective-permute-start(bf16[64,1280]{1,0:T(8,128)(2,1)S(1)} %convolution_convert_fusion.80), channel_id=1, source_target_pairs={{0,2},{1,3},{2,0},{3,1},{4,6},{5,7},{6,4},{7,5},{8,10},{9,11},{10,... | collective-permute-start | bytes 491528 | tf_op jit(solution)/shard_map/while/body/ppermute | solution.py:38
  82.9 9.7 %collective-permute-start.26 = (bf16[640,1792]{1,0:T(8,128)(2,1)S(1)}, bf16[640,1792]{1,0:T(8,128)(2,1)S(1)}, u32[]{:S(2)}, u32[]{:S(2)}) collective-permute-start(bf16[640,1792]{1,0:T(8,128)(2,1)S(1)} %constant_dynamic-update-slice_fusion.67), channel_id=1, source_target_pairs={{0,4},{4,0},{8,12},{12,8},{16,20},{20,16},{24,28},{28,24},{1,5},{5... | collective-permute-start | bytes 6881288 | tf_op jit(solution)/shard_map/while/body/ppermute | solution.py:44
  83.4 20.7 %collective-permute-start.21 = (bf16[160,1280]{1,0:T(8,128)(2,1)S(1)}, bf16[160,1280]{1,0:T(8,128)(2,1)S(1)}, u32[]{:S(2)}, u32[]{:S(2)}) collective-permute-start(bf16[160,1280]{1,0:T(8,128)(2,1)S(1)} %convolution_convert_fusion.88), channel_id=1, source_target_pairs={{0,16},{4,20},{8,24},{12,28},{16,0},{20,4},{24,8},{28,12},{1,17},{... | collective-permute-start | bytes 1228808 | tf_op jit(solution)/shard_map/while/body/ppermute | solution.py:44
  85.2 18.8 %collective-permute-start.22 = (bf16[160,1280]{1,0:T(8,128)(2,1)S(1)}, bf16[160,1280]{1,0:T(8,128)(2,1)S(1)}, u32[]{:S(2)}, u32[]{:S(2)}) collective-permute-start(bf16[160,1280]{1,0:T(8,128)(2,1)S(1)} %convolution_convert_fusion.89), channel_id=1, source_target_pairs={{0,24},{4,28},{8,16},{12,20},{16,8},{20,12},{24,0},{28,4},{1,25},{... | collective-permute-start | bytes 1228808 | tf_op jit(solution)/shard_map/while/body/ppermute | solution.py:44
  86.7 18.9 %collective-permute-start.20 = (bf16[160,1280]{1,0:T(8,128)(2,1)S(1)}, bf16[160,1280]{1,0:T(8,128)(2,1)S(1)}, u32[]{:S(2)}, u32[]{:S(2)}) collective-permute-start(bf16[160,1280]{1,0:T(8,128)(2,1)S(1)} %convolution_convert_fusion.87), channel_id=1, source_target_pairs={{0,8},{4,12},{8,0},{12,4},{16,24},{20,28},{24,16},{28,20},{1,9},{5... | collective-permute-start | bytes 1228808 | tf_op jit(solution)/shard_map/while/body/ppermute | solution.py:44
  126.7 11.3 %collective-permute-start.29 = (bf16[176,1024]{1,0:T(8,128)(2,1)S(1)}, bf16[176,1024]{1,0:T(8,128)(2,1)S(1)}, u32[]{:S(2)}, u32[]{:S(2)}) collective-permute-start(bf16[176,1024]{1,0:T(8,128)(2,1)S(1)} %get-tuple-element.487), channel_id=1, source_target_pairs={{0,8},{4,12},{8,0},{12,4},{16,24},{20,28},{24,16},{28,20},{1,9},{5... | collective-permute-start | bytes 1081352 | tf_op jit(solution)/shard_map/while/body/ppermute | solution.py:44
  127.9 16.3 %collective-permute-start.30 = (bf16[176,1024]{1,0:T(8,128)(2,1)S(1)}, bf16[176,1024]{1,0:T(8,128)(2,1)S(1)}, u32[]{:S(2)}, u32[]{:S(2)}) collective-permute-start(bf16[176,1024]{1,0:T(8,128)(2,1)S(1)} %get-tuple-element.488), channel_id=1, source_target_pairs={{0,16},{4,20},{8,24},{12,28},{16,0},{20,4},{24,8},{28,12},{1,17},{... | collective-permute-start | bytes 1081352 | tf_op jit(solution)/shard_map/while/body/ppermute | solution.py:44
  128.8 17.1 %collective-permute-start.31 = (bf16[176,1024]{1,0:T(8,128)(2,1)S(1)}, bf16[176,1024]{1,0:T(8,128)(2,1)S(1)}, u32[]{:S(2)}, u32[]{:S(2)}) collective-permute-start(bf16[176,1024]{1,0:T(8,128)(2,1)S(1)} %get-tuple-element.489), channel_id=1, source_target_pairs={{0,24},{4,28},{8,16},{12,20},{16,8},{20,12},{24,0},{28,4},{1,25},{... | collective-permute-start | bytes 1081352 | tf_op jit(solution)/shard_map/while/body/ppermute | solution.py:44
  148.7 9.7 %collective-permute-start.37 = (bf16[64,1024]{1,0:T(8,128)(2,1)S(1)}, bf16[64,1024]{1,0:T(8,128)(2,1)S(1)}, u32[]{:S(2)}, u32[]{:S(2)}) collective-permute-start(bf16[64,1024]{1,0:T(8,128)(2,1)S(1)} %get-tuple-element.507), channel_id=1, source_target_pairs={{0,3},{1,0},{2,1},{3,2},{4,7},{5,4},{6,5},{7,6},{8,11},{9,8},{10,9... | collective-permute-start | bytes 393224 | tf_op jit(solution)/shard_map/while/body/ppermute | solution.py:38
  148.7 12.8 %collective-permute-start.38 = (bf16[64,1024]{1,0:T(8,128)(2,1)S(1)}, bf16[64,1024]{1,0:T(8,128)(2,1)S(1)}, u32[]{:S(2)}, u32[]{:S(2)}) collective-permute-start(bf16[64,1024]{1,0:T(8,128)(2,1)S(1)} %get-tuple-element.508), channel_id=1, source_target_pairs={{0,2},{1,3},{2,0},{3,1},{4,6},{5,7},{6,4},{7,5},{8,10},{9,11},{10,... | collective-permute-start | bytes 393224 | tf_op jit(solution)/shard_map/while/body/ppermute | solution.py:38
  152.2 17.1 %collective-permute-start.33 = (bf16[176,1792]{1,0:T(8,128)(2,1)S(1)}, bf16[176,1792]{1,0:T(8,128)(2,1)S(1)}, u32[]{:S(2)}, u32[]{:S(2)}) collective-permute-start(bf16[176,1792]{1,0:T(8,128)(2,1)S(1)} %get-tuple-element.497), channel_id=1, source_target_pairs={{0,8},{4,12},{8,0},{12,4},{16,24},{20,28},{24,16},{28,20},{1,9},{5... | collective-permute-start | bytes 1892360 | tf_op jit(solution)/shard_map/while/body/ppermute | solution.py:44
  153.0 29.3 %collective-permute-start.34 = (bf16[176,1792]{1,0:T(8,128)(2,1)S(1)}, bf16[176,1792]{1,0:T(8,128)(2,1)S(1)}, u32[]{:S(2)}, u32[]{:S(2)}) collective-permute-start(bf16[176,1792]{1,0:T(8,128)(2,1)S(1)} %get-tuple-element.498), channel_id=1, source_target_pairs={{0,16},{4,20},{8,24},{12,28},{16,0},{20,4},{24,8},{28,12},{1,17},{... | collective-permute-start | bytes 1892360 | tf_op jit(solution)/shard_map/while/body/ppermute | solution.py:44
  156.0 26.3 %collective-permute-start.35 = (bf16[176,1792]{1,0:T(8,128)(2,1)S(1)}, bf16[176,1792]{1,0:T(8,128)(2,1)S(1)}, u32[]{:S(2)}, u32[]{:S(2)}) collective-permute-start(bf16[176,1792]{1,0:T(8,128)(2,1)S(1)} %get-tuple-element.499), channel_id=1, source_target_pairs={{0,24},{4,28},{8,16},{12,20},{16,8},{20,12},{24,0},{28,4},{1,25},{... | collective-permute-start | bytes 1892360 | tf_op jit(solution)/shard_map/while/body/ppermute | solution.py:44
  185.7 20.0 %collective-permute-start.40 = (bf16[176,1280]{1,0:T(8,128)(2,1)S(1)}, bf16[176,1280]{1,0:T(8,128)(2,1)}, u32[]{:S(2)}, u32[]{:S(2)}) collective-permute-start(bf16[176,1280]{1,0:T(8,128)(2,1)S(1)} %get-tuple-element.512), channel_id=1, source_target_pairs={{0,8},{4,12},{8,0},{12,4},{16,24},{20,28},{24,16},{28,20},{1,9},{5... | collective-permute-start | bytes 1351688 | tf_op jit(solution)/shard_map/while/body/ppermute | solution.py:44
  186.9 20.7 %collective-permute-start.41 = (bf16[176,1280]{1,0:T(8,128)(2,1)S(1)}, bf16[176,1280]{1,0:T(8,128)(2,1)}, u32[]{:S(2)}, u32[]{:S(2)}) collective-permute-start(bf16[176,1280]{1,0:T(8,128)(2,1)S(1)} %get-tuple-element.513), channel_id=1, source_target_pairs={{0,16},{4,20},{8,24},{12,28},{16,0},{20,4},{24,8},{28,12},{1,17},{... | collective-permute-start | bytes 1351688 | tf_op jit(solution)/shard_map/while/body/ppermute | solution.py:44
  187.8 19.8 %collective-permute-start.42 = (bf16[176,1280]{1,0:T(8,128)(2,1)S(1)}, bf16[176,1280]{1,0:T(8,128)(2,1)}, u32[]{:S(2)}, u32[]{:S(2)}) collective-permute-start(bf16[176,1280]{1,0:T(8,128)(2,1)S(1)} %get-tuple-element.514), channel_id=1, source_target_pairs={{0,24},{4,28},{8,16},{12,20},{16,8},{20,12},{24,0},{28,4},{1,25},{... | collective-permute-start | bytes 1351688 | tf_op jit(solution)/shard_map/while/body/ppermute | solution.py:44
  189.2 16.4 %collective-permute-start.44 = (bf16[64,1792]{1,0:T(8,128)(2,1)}, bf16[64,1792]{1,0:T(8,128)(2,1)}, u32[]{:S(2)}, u32[]{:S(2)}) collective-permute-start(bf16[64,1792]{1,0:T(8,128)(2,1)} %get-tuple-element.525), channel_id=1, source_target_pairs={{0,2},{1,3},{2,0},{3,1},{4,6},{5,7},{6,4},{7,5},{8,10},{9,11},{10,... | collective-permute-start | bytes 688136 | tf_op jit(solution)/shard_map/while/body/ppermute | solution.py:38
  192.1 13.6 %collective-permute-start.45 = (bf16[64,1792]{1,0:T(8,128)(2,1)}, bf16[64,1792]{1,0:T(8,128)(2,1)}, u32[]{:S(2)}, u32[]{:S(2)}) collective-permute-start(bf16[64,1792]{1,0:T(8,128)(2,1)} %get-tuple-element.526), channel_id=1, source_target_pairs={{0,1},{1,2},{2,3},{3,0},{4,5},{5,6},{6,7},{7,4},{8,9},{9,10},{10,1... | collective-permute-start | bytes 688136 | tf_op jit(solution)/shard_map/while/body/ppermute | solution.py:38
  210.5 11.9 %collective-permute-start.47 = (bf16[64,1280]{1,0:T(8,128)(2,1)S(1)}, bf16[64,1280]{1,0:T(8,128)(2,1)S(1)}, u32[]{:S(2)}, u32[]{:S(2)}) collective-permute-start(bf16[64,1280]{1,0:T(8,128)(2,1)S(1)} %get-tuple-element.532), channel_id=1, source_target_pairs={{0,2},{1,3},{2,0},{3,1},{4,6},{5,7},{6,4},{7,5},{8,10},{9,11},{10,... | collective-permute-start | bytes 491528 | tf_op jit(solution)/shard_map/while/body/ppermute | solution.py:38
  211.1 11.3 %collective-permute-start.48 = (bf16[64,1280]{1,0:T(8,128)(2,1)S(1)}, bf16[64,1280]{1,0:T(8,128)(2,1)S(1)}, u32[]{:S(2)}, u32[]{:S(2)}) collective-permute-start(bf16[64,1280]{1,0:T(8,128)(2,1)S(1)} %get-tuple-element.533), channel_id=1, source_target_pairs={{0,3},{1,0},{2,1},{3,2},{4,7},{5,4},{6,5},{7,6},{8,11},{9,8},{10,9... | collective-permute-start | bytes 491528 | tf_op jit(solution)/shard_map/while/body/ppermute | solution.py:38
  (33 other events, 224.6 us)

commit v2 on v1

--- a/solution.py
+++ b/solution.py
@@ -163,7 +163,7 @@
     n_rep, n_exp, rows, cap, cap_back, cap_z, cap_z_back = sizes
     group = rows * n_exp
     n_pair = n_rep // 2
-    high, low = refs[n_pair:]
+    table_out = refs[n_pair]
     my_rep = place[0]
     my_exp = place[1]
     in_group = before_table(group, group)
@@ -181,10 +181,9 @@
         target = slots_of(code_back, cap_back).astype(jnp.float32)
         for at, expert in enumerate((own, other)):
             weight = jnp.sum(jnp.where(named == expert, weights, 0.0), axis=0, keepdims=True)
-            weight_high = weight.astype(BF16).astype(jnp.float32)
-            for out, value in ((high, weight_high), (low, weight - weight_high)):
-                table = dot_nt((target * value).astype(BF16), source).astype(BF16)
-                out[k, :, at * cap : (at + 1) * cap] = table
+            table_out[k, :, at * cap : (at + 1) * cap] = dot_nt(
+                (target * weight).astype(BF16), source
+            ).astype(BF16)
 
 
 def plan_call(body, shapes, place, *tables):
@@ -268,9 +267,9 @@
         sent, facts = lax.optimization_barrier((packed(in_cols[0], shared), facts))
         held = along_exp(sent)
         served = [flip(facts, n_rep, 2 * k) for k in range(n_pair)]
-        high, low = plan_call(
+        (high,) = plan_call(
             functools.partial(pair_plan, sizes),
-            [((n_pair, cap_back, 2 * cap), BF16)] * 2,
+            [((n_pair, cap_back, 2 * cap), BF16)],
             place,
             *served,
         )
@@ -283,8 +282,8 @@
         sums = (0.0, 0.0, 0.0, 0.0)
         for part, cols in enumerate(in_cols):
             if part < last:
-                held, shared, sums, high, low, fits = lax.optimization_barrier(
-                    (held, shared, sums, high, low, fits)
+                held, shared, sums, high, fits = lax.optimization_barrier(
+                    (held, shared, sums, high, fits)
                 )
                 after = to_pairs(held)
                 if part + 1 < last:
@@ -308,7 +307,6 @@
                 [own.reshape(n_pair, cap, -1), given.reshape(n_pair, cap, -1)], axis=1
             )
             total = jnp.einsum("krs,ksd->krd", high, both, preferred_element_type=jnp.float32)
-            total += jnp.einsum("krs,ksd->krd", low, both, preferred_element_type=jnp.float32)
             totals = total.astype(BF16)
             return totals
 

time: 227 us -> 222 us (0.978)
  matrix products: 53 us -> 44.4 us
  starting transfers between devices: 55.1 us -> 58.4 us
    dot_general x45, matrix products: 43.3 us -> 38.8 us  [dot(): return jnp.dot(a, b, preferred_element_type=jnp.float32)]
    dot_general x3 -> x0, matrix products: 3.48 us -> none  [weighted(): jnp.einsum('krs,ksd->krd', low, both, preferred_element_type=jnp.float32)]
    ppermute x21, starting transfers between devices: 29.4 us -> 32.7 us  [ring(): lax.ppermute(value, axis, [(i, (i + shift) % size) for i in range(size)])]
  transfers between devices with their start and end apart: 49 -> 49, of which waited for: 20 -> 19; matrix products, arithmetic and copies ran while one was open for 19% -> 17% of each run, Pallas kernels for 2% -> 2%
where the time goes in v2:
time: 222 us; the launch traced here: 221 us
  waiting for transfers between devices  94.4 us (43%)
  starting transfers between devices  58.4 us (26%)
  matrix products  44.4 us (20%)
  other arithmetic  7.17 us (3%)
  Pallas kernels  6.6 us (3%)
  local copies, waits for them, and re-layouts  6.28 us (3%)
  loops' own time  3.17 us (1%)
    ppermute x21, waiting for transfers between devices, ring(): lax.ppermute(value, axis, [(i, (i + shift) % size) for i in range(size)])  50.2 us
    ppermute x28, waiting for transfers between devices, flip(): return lax.ppermute(value, 'rep', [(i, i ^ mask) for i in range(size)])  44.1 us
    dot_general x45, matrix products, dot(): return jnp.dot(a, b, preferred_element_type=jnp.float32)  38.8 us
    ppermute x21, starting transfers between devices, ring(): lax.ppermute(value, axis, [(i, (i + shift) % size) for i in range(size)])  32.7 us
    ppermute x28, starting transfers between devices, flip(): return lax.ppermute(value, 'rep', [(i, i ^ mask) for i in range(size)])  25.6 us
    pallas_call x3, Pallas kernels, plan_call(): pl.pallas_call(body, out_shape=[jax.ShapeDtypeStruct(shape, kind) for sha...  6.6 us
  transfers between devices with their start and end apart: 49, of which 19 were waited for; matrix products, arithmetic and copies ran while one was open for 17% of the time, Pallas kernels for 2%

profile of v2, /device:TPU:0, one launch (start us, length us, event | category | flops | bytes accessed | tf_op | source)
XLA Modules:
  0.0 220.6 jit_solution(17782564016753344595)
XLA Ops:
  0.2 219.2 %while.12 = (s32[]{:T(128)}, s32[]{:T(128)}, bf16[128,4096]{1,0:T(8,128)(2,1)S(1)}, s32[1]{0:T(128)}, s32[128,8]{0,1:T(8,128)}, /*index=5*/f32[128,8]{0,1:T(8,12...) while((s32[]{:T(128)}, s32[]{:T(128)}, ...), condition=%wide.region_2.3_spmd, body=%wide.region_0.2_spmd.sunk | while | flops 29446639616 | bytes 378171840 | solution.py:346
  2.2 3.1 %collective-permute-start = (f32[24,128]{1,0:T(8,128)S(1)}, f32[24,128]{1,0:T(8,128)S(1)}, u32[]{:S(2)}, u32[]{:S(2)}) collective-permute-start(f32[24,128]{1,0:T(8,128)S(1)} %body.3.refs_0_), channel_id=1, source_target_pairs={{0,1},{1,2},{2,3},{3,0},{4,5},{5,6},{6,7},{7,4},{8,9},{9,10},{10,1... | collective-permute-start | bytes 36872 | tf_op jit(solution)/shard_map/while/body/ppermute | solution.py:38
  5.3 2.6 %collective-permute-start.1 = (f32[24,128]{1,0:T(8,128)S(1)}, f32[24,128]{1,0:T(8,128)S(1)}, u32[]{:S(2)}, u32[]{:S(2)}) collective-permute-start(f32[24,128]{1,0:T(8,128)S(1)} %body.3.refs_0_), channel_id=1, source_target_pairs={{0,2},{1,3},{2,0},{3,1},{4,6},{5,7},{6,4},{7,5},{8,10},{9,11},{10,... | collective-permute-start | bytes 36872 | tf_op jit(solution)/shard_map/while/body/ppermute | solution.py:38
  12.3 2.2 body.4
  19.6 2.3 %collective-permute-start.14 = (bf16[64,1024]{1,0:T(8,128)(2,1)S(1)}, bf16[64,1024]{1,0:T(8,128)(2,1)S(1)}, u32[]{:S(2)}, u32[]{:S(2)}) collective-permute-start(bf16[64,1024]{1,0:T(8,128)(2,1)S(1)} %convolution_convert_fusion.74), channel_id=1, source_target_pairs={{0,2},{1,3},{2,0},{3,1},{4,6},{5,7},{6,4},{7,5},{8,10},{9,11},{10,... | collective-permute-start | bytes 393224 | tf_op jit(solution)/shard_map/while/body/ppermute | solution.py:38
  23.3 3.6 %body.5 = bf16[4,176,320]{2,1,0:T(8,128)(2,1)S(1)} custom-call(s32[2]{0:T(128)S(1)} %get-tuple-element.575.place, f32[24,512]{1,0:T(8,128)S(1)} %get-tuple-element.418.refs_0_, f32[24,512]{1,0:T(8,128)S(1)} %collective-permute-done.3.refs_1_, f32[24,512]{1,0:T(8,128)S(1)} %collective-permute-done.4.refs_2_, f32[24,512]{1,0:T(8,128)S(1)} %collective-permute-done.5.refs_3_), custom_call_target="tpu_custom_call" | custom-call | tf_op jit(solution)/shard_map/while/body/pallas_call | solution.py:191
  27.9 2.4 %collective-permute-start.8 = (bf16[64,1792]{1,0:T(8,128)(2,1)S(1)}, bf16[64,1792]{1,0:T(8,128)(2,1)S(1)}, u32[]{:S(2)}, u32[]{:S(2)}) collective-permute-start(bf16[64,1792]{1,0:T(8,128)(2,1)S(1)} %convolution_convert_fusion.79), channel_id=1, source_target_pairs={{0,3},{1,0},{2,1},{3,2},{4,7},{5,4},{6,5},{7,6},{8,11},{9,8},{10,9... | collective-permute-start | bytes 688136 | tf_op jit(solution)/shard_map/while/body/ppermute | solution.py:38
  32.6 2.1 collective-permute-start.18
  36.8 15.0 %collective-permute-done.7 = bf16[64,1792]{1,0:T(8,128)(2,1)S(1)} collective-permute-done((bf16[64,1792]{1,0:T(8,128)(2,1)S(1)}, bf16[64,1792]{1,0:T(8,128)(2,1)S(1)}, u32[]{:S(2)}, u32[]{:S(2)}) %collective-permute-start.7) | collective-permute-done | bytes 229408 | tf_op jit(solution)/shard_map/while/body/ppermute | solution.py:38
  61.9 3.4 %collective-permute-start.11 = (bf16[64,1280]{1,0:T(8,128)(2,1)S(1)}, bf16[64,1280]{1,0:T(8,128)(2,1)S(1)}, u32[]{:S(2)}, u32[]{:S(2)}) collective-permute-start(bf16[64,1280]{1,0:T(8,128)(2,1)S(1)} %convolution_convert_fusion.82), channel_id=1, source_target_pairs={{0,2},{1,3},{2,0},{3,1},{4,6},{5,7},{6,4},{7,5},{8,10},{9,11},{10,... | collective-permute-start | bytes 491528 | tf_op jit(solution)/shard_map/while/body/ppermute | solution.py:38
  68.2 7.8 %collective-permute-done.11 = bf16[64,1280]{1,0:T(8,128)(2,1)S(1)} collective-permute-done((bf16[64,1280]{1,0:T(8,128)(2,1)S(1)}, bf16[64,1280]{1,0:T(8,128)(2,1)S(1)}, u32[]{:S(2)}, u32[]{:S(2)}) %collective-permute-start.11) | collective-permute-done | bytes 163872 | tf_op jit(solution)/shard_map/while/body/ppermute | solution.py:38
  76.0 6.7 %collective-permute-done.24 = bf16[160,1792]{1,0:T(8,128)(2,1)S(1)} collective-permute-done((bf16[160,1792]{1,0:T(8,128)(2,1)S(1)}, bf16[160,1792]{1,0:T(8,128)(2,1)S(1)}, u32[]{:S(2)}, u32[]{:S(2)}) %collective-permute-start.24) | collective-permute-done | bytes 573472 | tf_op jit(solution)/shard_map/while/body/ppermute | solution.py:44
  87.6 2.0 fusion.416
  90.0 2.0 fusion.415
  92.6 2.0 fusion.418
  95.0 2.0 fusion.417
  97.3 6.7 %collective-permute-done.21 = bf16[160,1280]{1,0:T(8,128)(2,1)S(1)} collective-permute-done((bf16[160,1280]{1,0:T(8,128)(2,1)S(1)}, bf16[160,1280]{1,0:T(8,128)(2,1)S(1)}, u32[]{:S(2)}, u32[]{:S(2)}) %collective-permute-start.21) | collective-permute-done | bytes 409632 | tf_op jit(solution)/shard_map/while/body/ppermute | solution.py:44
  107.3 2.0 collective-permute-done.27
  113.1 2.8 %convolution_convert_fusion.96 = bf16[640,1024]{1,0:T(8,128)(2,1)S(1)} fusion(bf16[640,768]{1,0:T(8,128)(2,1)S(1)} %multiply_convert_fusion.4, bf16[1,768,4096]{2,1,0:T(8,128)(2,1)} %get-tuple-element.579), kind=kOutput, calls=%fused_computation.91.clone.1 | convolution fusion | flops 1007288320 | bytes 3866624 | tf_op jit(solution)/shard_map/while/body/dot_general | solution.py:20
  126.4 2.0 convolution_convert_fusion.99
  130.1 4.1 %collective-permute-done.29 = bf16[176,1024]{1,0:T(8,128)(2,1)S(1)} collective-permute-done((bf16[176,1024]{1,0:T(8,128)(2,1)S(1)}, bf16[176,1024]{1,0:T(8,128)(2,1)S(1)}, u32[]{:S(2)}, u32[]{:S(2)}) %collective-permute-start.29) | collective-permute-done | bytes 360480 | tf_op jit(solution)/shard_map/while/body/ppermute | solution.py:44
  134.1 6.2 %collective-permute-done.30 = bf16[176,1024]{1,0:T(8,128)(2,1)S(1)} collective-permute-done((bf16[176,1024]{1,0:T(8,128)(2,1)S(1)}, bf16[176,1024]{1,0:T(8,128)(2,1)S(1)}, u32[]{:S(2)}, u32[]{:S(2)}) %collective-permute-start.30) | collective-permute-done | bytes 360480 | tf_op jit(solution)/shard_map/while/body/ppermute | solution.py:44
  151.2 2.6 %collective-permute-start.38 = (bf16[64,1024]{1,0:T(8,128)(2,1)S(1)}, bf16[64,1024]{1,0:T(8,128)(2,1)S(1)}, u32[]{:S(2)}, u32[]{:S(2)}) collective-permute-start(bf16[64,1024]{1,0:T(8,128)(2,1)S(1)} %get-tuple-element.496), channel_id=1, source_target_pairs={{0,2},{1,3},{2,0},{3,1},{4,6},{5,7},{6,4},{7,5},{8,10},{9,11},{10,... | collective-permute-start | bytes 393224 | tf_op jit(solution)/shard_map/while/body/ppermute | solution.py:38
  154.9 8.1 %collective-permute-done.38 = bf16[64,1024]{1,0:T(8,128)(2,1)S(1)} collective-permute-done((bf16[64,1024]{1,0:T(8,128)(2,1)S(1)}, bf16[64,1024]{1,0:T(8,128)(2,1)S(1)}, u32[]{:S(2)}, u32[]{:S(2)}) %collective-permute-start.38) | collective-permute-done | bytes 131104 | tf_op jit(solution)/shard_map/while/body/ppermute | solution.py:38
  163.0 13.1 %collective-permute-done.34 = bf16[176,1792]{1,0:T(8,128)(2,1)S(1)} collective-permute-done((bf16[176,1792]{1,0:T(8,128)(2,1)S(1)}, bf16[176,1792]{1,0:T(8,128)(2,1)S(1)}, u32[]{:S(2)}, u32[]{:S(2)}) %collective-permute-start.34) | collective-permute-done | bytes 630816 | tf_op jit(solution)/shard_map/while/body/ppermute | solution.py:44
  178.1 2.3 %collective-permute-start.43 = (bf16[64,1792]{1,0:T(8,128)(2,1)S(1)}, bf16[64,1792]{1,0:T(8,128)(2,1)S(1)}, u32[]{:S(2)}, u32[]{:S(2)}) collective-permute-start(bf16[64,1792]{1,0:T(8,128)(2,1)S(1)} %get-tuple-element.512), channel_id=1, source_target_pairs={{0,3},{1,0},{2,1},{3,2},{4,7},{5,4},{6,5},{7,6},{8,11},{9,8},{10,9... | collective-permute-start | bytes 688136 | tf_op jit(solution)/shard_map/while/body/ppermute | solution.py:38
  186.2 3.2 %collective-permute-start.45 = (bf16[64,1792]{1,0:T(8,128)(2,1)}, bf16[64,1792]{1,0:T(8,128)(2,1)}, u32[]{:S(2)}, u32[]{:S(2)}) collective-permute-start(bf16[64,1792]{1,0:T(8,128)(2,1)} %get-tuple-element.514), channel_id=1, source_target_pairs={{0,1},{1,2},{2,3},{3,0},{4,5},{5,6},{6,7},{7,4},{8,9},{9,10},{10,1... | collective-permute-start | bytes 688136 | tf_op jit(solution)/shard_map/while/body/ppermute | solution.py:38
  190.7 10.4 %collective-permute-done.44 = bf16[64,1792]{1,0:T(8,128)(2,1)} collective-permute-done((bf16[64,1792]{1,0:T(8,128)(2,1)}, bf16[64,1792]{1,0:T(8,128)(2,1)}, u32[]{:S(2)}, u32[]{:S(2)}) %collective-permute-start.44) | collective-permute-done | bytes 229408 | tf_op jit(solution)/shard_map/while/body/ppermute | solution.py:38
  202.5 2.0 convolution_convert_fusion.104
  204.9 2.7 %collective-permute-start.47 = (bf16[64,1280]{1,0:T(8,128)(2,1)S(1)}, bf16[64,1280]{1,0:T(8,128)(2,1)S(1)}, u32[]{:S(2)}, u32[]{:S(2)}) collective-permute-start(bf16[64,1280]{1,0:T(8,128)(2,1)S(1)} %get-tuple-element.520), channel_id=1, source_target_pairs={{0,2},{1,3},{2,0},{3,1},{4,6},{5,7},{6,4},{7,5},{8,10},{9,11},{10,... | collective-permute-start | bytes 491528 | tf_op jit(solution)/shard_map/while/body/ppermute | solution.py:38
  210.6 3.0 %collective-permute-done.46 = bf16[64,1280]{1,0:T(8,128)(2,1)S(1)} collective-permute-done((bf16[64,1280]{1,0:T(8,128)(2,1)S(1)}, bf16[64,1280]{1,0:T(8,128)(2,1)S(1)}, u32[]{:S(2)}, u32[]{:S(2)}) %collective-permute-start.46) | collective-permute-done | bytes 163872 | tf_op jit(solution)/shard_map/while/body/ppermute | solution.py:38
  213.6 4.0 %collective-permute-done.47 = bf16[64,1280]{1,0:T(8,128)(2,1)S(1)} collective-permute-done((bf16[64,1280]{1,0:T(8,128)(2,1)S(1)}, bf16[64,1280]{1,0:T(8,128)(2,1)S(1)}, u32[]{:S(2)}, u32[]{:S(2)}) %collective-permute-start.47) | collective-permute-done | bytes 163872 | tf_op jit(solution)/shard_map/while/body/ppermute | solution.py:38
  (202 shorter events, 83.0 us)
Async XLA Ops:
  2.2 10.1 %collective-permute-start = (f32[24,128]{1,0:T(8,128)S(1)}, f32[24,128]{1,0:T(8,128)S(1)}, u32[]{:S(2)}, u32[]{:S(2)}) collective-permute-start(f32[24,128]{1,0:T(8,128)S(1)} %body.3.refs_0_), channel_id=1, source_target_pairs={{0,1},{1,2},{2,3},{3,0},{4,5},{5,6},{6,7},{7,4},{8,9},{9,10},{10,1... | collective-permute-start | bytes 36872 | tf_op jit(solution)/shard_map/while/body/ppermute | solution.py:38
  18.8 11.5 %collective-permute-start.13 = (bf16[64,1024]{1,0:T(8,128)(2,1)S(1)}, bf16[64,1024]{1,0:T(8,128)(2,1)S(1)}, u32[]{:S(2)}, u32[]{:S(2)}) collective-permute-start(bf16[64,1024]{1,0:T(8,128)(2,1)S(1)} %convolution_convert_fusion.73), channel_id=1, source_target_pairs={{0,1},{1,2},{2,3},{3,0},{4,5},{5,6},{6,7},{7,4},{8,9},{9,10},{10,1... | collective-permute-start | bytes 393224 | tf_op jit(solution)/shard_map/while/body/ppermute | solution.py:38
  19.6 12.2 %collective-permute-start.14 = (bf16[64,1024]{1,0:T(8,128)(2,1)S(1)}, bf16[64,1024]{1,0:T(8,128)(2,1)S(1)}, u32[]{:S(2)}, u32[]{:S(2)}) collective-permute-start(bf16[64,1024]{1,0:T(8,128)(2,1)S(1)} %convolution_convert_fusion.74), channel_id=1, source_target_pairs={{0,2},{1,3},{2,0},{3,1},{4,6},{5,7},{6,4},{7,5},{8,10},{9,11},{10,... | collective-permute-start | bytes 393224 | tf_op jit(solution)/shard_map/while/body/ppermute | solution.py:38
  21.8 10.0 %collective-permute-start.15 = (bf16[64,1024]{1,0:T(8,128)(2,1)S(1)}, bf16[64,1024]{1,0:T(8,128)(2,1)S(1)}, u32[]{:S(2)}, u32[]{:S(2)}) collective-permute-start(bf16[64,1024]{1,0:T(8,128)(2,1)S(1)} %convolution_convert_fusion.75), channel_id=1, source_target_pairs={{0,3},{1,0},{2,1},{3,2},{4,7},{5,4},{6,5},{7,6},{8,11},{9,8},{10,9... | collective-permute-start | bytes 393224 | tf_op jit(solution)/shard_map/while/body/ppermute | solution.py:38
  30.3 21.5 %collective-permute-start.7 = (bf16[64,1792]{1,0:T(8,128)(2,1)S(1)}, bf16[64,1792]{1,0:T(8,128)(2,1)S(1)}, u32[]{:S(2)}, u32[]{:S(2)}) collective-permute-start(bf16[64,1792]{1,0:T(8,128)(2,1)S(1)} %convolution_convert_fusion.78), channel_id=1, source_target_pairs={{0,2},{1,3},{2,0},{3,1},{4,6},{5,7},{6,4},{7,5},{8,10},{9,11},{10,... | collective-permute-start | bytes 688136 | tf_op jit(solution)/shard_map/while/body/ppermute | solution.py:38
  30.3 21.5 %collective-permute-start.6 = (bf16[64,1792]{1,0:T(8,128)(2,1)S(1)}, bf16[64,1792]{1,0:T(8,128)(2,1)S(1)}, u32[]{:S(2)}, u32[]{:S(2)}) collective-permute-start(bf16[64,1792]{1,0:T(8,128)(2,1)S(1)} %convolution_convert_fusion.77), channel_id=1, source_target_pairs={{0,1},{1,2},{2,3},{3,0},{4,5},{5,6},{6,7},{7,4},{8,9},{9,10},{10,1... | collective-permute-start | bytes 688136 | tf_op jit(solution)/shard_map/while/body/ppermute | solution.py:38
  32.6 20.7 %collective-permute-start.18 = (bf16[160,1024]{1,0:T(8,128)(2,1)S(1)}, bf16[160,1024]{1,0:T(8,128)(2,1)S(1)}, u32[]{:S(2)}, u32[]{:S(2)}) collective-permute-start(bf16[160,1024]{1,0:T(8,128)(2,1)S(1)} %convolution_convert_fusion.87), channel_id=1, source_target_pairs={{0,24},{4,28},{8,16},{12,20},{16,8},{20,12},{24,0},{28,4},{1,25},{... | collective-permute-start | bytes 983048 | tf_op jit(solution)/shard_map/while/body/ppermute | solution.py:44
  34.8 18.6 %collective-permute-start.17 = (bf16[160,1024]{1,0:T(8,128)(2,1)S(1)}, bf16[160,1024]{1,0:T(8,128)(2,1)S(1)}, u32[]{:S(2)}, u32[]{:S(2)}) collective-permute-start(bf16[160,1024]{1,0:T(8,128)(2,1)S(1)} %convolution_convert_fusion.86), channel_id=1, source_target_pairs={{0,16},{4,20},{8,24},{12,28},{16,0},{20,4},{24,8},{28,12},{1,17},{... | collective-permute-start | bytes 983048 | tf_op jit(solution)/shard_map/while/body/ppermute | solution.py:44
  36.3 17.0 %collective-permute-start.16 = (bf16[160,1024]{1,0:T(8,128)(2,1)S(1)}, bf16[160,1024]{1,0:T(8,128)(2,1)S(1)}, u32[]{:S(2)}, u32[]{:S(2)}) collective-permute-start(bf16[160,1024]{1,0:T(8,128)(2,1)S(1)} %convolution_convert_fusion.85), channel_id=1, source_target_pairs={{0,8},{4,12},{8,0},{12,4},{16,24},{20,28},{24,16},{28,20},{1,9},{5... | collective-permute-start | bytes 983048 | tf_op jit(solution)/shard_map/while/body/ppermute | solution.py:44
  53.8 22.2 %collective-permute-start.23 = (bf16[160,1792]{1,0:T(8,128)(2,1)S(1)}, bf16[160,1792]{1,0:T(8,128)(2,1)S(1)}, u32[]{:S(2)}, u32[]{:S(2)}) collective-permute-start(bf16[160,1792]{1,0:T(8,128)(2,1)S(1)} %convolution_convert_fusion.93), channel_id=1, source_target_pairs={{0,8},{4,12},{8,0},{12,4},{16,24},{20,28},{24,16},{28,20},{1,9},{5... | collective-permute-start | bytes 1720328 | tf_op jit(solution)/shard_map/while/body/ppermute | solution.py:44
  55.3 27.4 %collective-permute-start.24 = (bf16[160,1792]{1,0:T(8,128)(2,1)S(1)}, bf16[160,1792]{1,0:T(8,128)(2,1)S(1)}, u32[]{:S(2)}, u32[]{:S(2)}) collective-permute-start(bf16[160,1792]{1,0:T(8,128)(2,1)S(1)} %convolution_convert_fusion.94), channel_id=1, source_target_pairs={{0,16},{4,20},{8,24},{12,28},{16,0},{20,4},{24,8},{28,12},{1,17},{... | collective-permute-start | bytes 1720328 | tf_op jit(solution)/shard_map/while/body/ppermute | solution.py:44
  56.9 25.9 %collective-permute-start.25 = (bf16[160,1792]{1,0:T(8,128)(2,1)S(1)}, bf16[160,1792]{1,0:T(8,128)(2,1)S(1)}, u32[]{:S(2)}, u32[]{:S(2)}) collective-permute-start(bf16[160,1792]{1,0:T(8,128)(2,1)S(1)} %convolution_convert_fusion.95), channel_id=1, source_target_pairs={{0,24},{4,28},{8,16},{12,20},{16,8},{20,12},{24,0},{28,4},{1,25},{... | collective-permute-start | bytes 1720328 | tf_op jit(solution)/shard_map/while/body/ppermute | solution.py:44
  61.9 14.1 %collective-permute-start.11 = (bf16[64,1280]{1,0:T(8,128)(2,1)S(1)}, bf16[64,1280]{1,0:T(8,128)(2,1)S(1)}, u32[]{:S(2)}, u32[]{:S(2)}) collective-permute-start(bf16[64,1280]{1,0:T(8,128)(2,1)S(1)} %convolution_convert_fusion.82), channel_id=1, source_target_pairs={{0,2},{1,3},{2,0},{3,1},{4,6},{5,7},{6,4},{7,5},{8,10},{9,11},{10,... | collective-permute-start | bytes 491528 | tf_op jit(solution)/shard_map/while/body/ppermute | solution.py:38
  82.9 9.7 %collective-permute-start.26 = (bf16[640,1792]{1,0:T(8,128)(2,1)S(1)}, bf16[640,1792]{1,0:T(8,128)(2,1)S(1)}, u32[]{:S(2)}, u32[]{:S(2)}) collective-permute-start(bf16[640,1792]{1,0:T(8,128)(2,1)S(1)} %constant_dynamic-update-slice_fusion.67), channel_id=1, source_target_pairs={{0,4},{4,0},{8,12},{12,8},{16,20},{20,16},{24,28},{28,24},{1,5},{5... | collective-permute-start | bytes 6881288 | tf_op jit(solution)/shard_map/while/body/ppermute | solution.py:44
  83.4 20.7 %collective-permute-start.21 = (bf16[160,1280]{1,0:T(8,128)(2,1)S(1)}, bf16[160,1280]{1,0:T(8,128)(2,1)S(1)}, u32[]{:S(2)}, u32[]{:S(2)}) collective-permute-start(bf16[160,1280]{1,0:T(8,128)(2,1)S(1)} %convolution_convert_fusion.90), channel_id=1, source_target_pairs={{0,16},{4,20},{8,24},{12,28},{16,0},{20,4},{24,8},{28,12},{1,17},{... | collective-permute-start | bytes 1228808 | tf_op jit(solution)/shard_map/while/body/ppermute | solution.py:44
  85.2 18.8 %collective-permute-start.22 = (bf16[160,1280]{1,0:T(8,128)(2,1)S(1)}, bf16[160,1280]{1,0:T(8,128)(2,1)S(1)}, u32[]{:S(2)}, u32[]{:S(2)}) collective-permute-start(bf16[160,1280]{1,0:T(8,128)(2,1)S(1)} %convolution_convert_fusion.91), channel_id=1, source_target_pairs={{0,24},{4,28},{8,16},{12,20},{16,8},{20,12},{24,0},{28,4},{1,25},{... | collective-permute-start | bytes 1228808 | tf_op jit(solution)/shard_map/while/body/ppermute | solution.py:44
  86.7 18.9 %collective-permute-start.20 = (bf16[160,1280]{1,0:T(8,128)(2,1)S(1)}, bf16[160,1280]{1,0:T(8,128)(2,1)S(1)}, u32[]{:S(2)}, u32[]{:S(2)}) collective-permute-start(bf16[160,1280]{1,0:T(8,128)(2,1)S(1)} %convolution_convert_fusion.89), channel_id=1, source_target_pairs={{0,8},{4,12},{8,0},{12,4},{16,24},{20,28},{24,16},{28,20},{1,9},{5... | collective-permute-start | bytes 1228808 | tf_op jit(solution)/shard_map/while/body/ppermute | solution.py:44
  122.8 11.3 %collective-permute-start.29 = (bf16[176,1024]{1,0:T(8,128)(2,1)S(1)}, bf16[176,1024]{1,0:T(8,128)(2,1)S(1)}, u32[]{:S(2)}, u32[]{:S(2)}) collective-permute-start(bf16[176,1024]{1,0:T(8,128)(2,1)S(1)} %get-tuple-element.475), channel_id=1, source_target_pairs={{0,8},{4,12},{8,0},{12,4},{16,24},{20,28},{24,16},{28,20},{1,9},{5... | collective-permute-start | bytes 1081352 | tf_op jit(solution)/shard_map/while/body/ppermute | solution.py:44
  124.1 16.3 %collective-permute-start.30 = (bf16[176,1024]{1,0:T(8,128)(2,1)S(1)}, bf16[176,1024]{1,0:T(8,128)(2,1)S(1)}, u32[]{:S(2)}, u32[]{:S(2)}) collective-permute-start(bf16[176,1024]{1,0:T(8,128)(2,1)S(1)} %get-tuple-element.476), channel_id=1, source_target_pairs={{0,16},{4,20},{8,24},{12,28},{16,0},{20,4},{24,8},{28,12},{1,17},{... | collective-permute-start | bytes 1081352 | tf_op jit(solution)/shard_map/while/body/ppermute | solution.py:44
  124.9 17.1 %collective-permute-start.31 = (bf16[176,1024]{1,0:T(8,128)(2,1)S(1)}, bf16[176,1024]{1,0:T(8,128)(2,1)S(1)}, u32[]{:S(2)}, u32[]{:S(2)}) collective-permute-start(bf16[176,1024]{1,0:T(8,128)(2,1)S(1)} %get-tuple-element.477), channel_id=1, source_target_pairs={{0,24},{4,28},{8,16},{12,20},{16,8},{20,12},{24,0},{28,4},{1,25},{... | collective-permute-start | bytes 1081352 | tf_op jit(solution)/shard_map/while/body/ppermute | solution.py:44
  143.5 10.3 %collective-permute-start.36 = (bf16[640,1280]{1,0:T(8,128)(2,1)S(1)}, bf16[640,1280]{1,0:T(8,128)(2,1)S(1)}, u32[]{:S(2)}, u32[]{:S(2)}) collective-permute-start(bf16[640,1280]{1,0:T(8,128)(2,1)S(1)} %convolution_convert_fusion.100), channel_id=1, source_target_pairs={{0,4},{4,0},{8,12},{12,8},{16,20},{20,16},{24,28},{28,24},{1,5},{5... | collective-permute-start | bytes 4915208 | tf_op jit(solution)/shard_map/while/body/ppermute | solution.py:44
  145.4 17.6 %collective-permute-start.33 = (bf16[176,1792]{1,0:T(8,128)(2,1)S(1)}, bf16[176,1792]{1,0:T(8,128)(2,1)S(1)}, u32[]{:S(2)}, u32[]{:S(2)}) collective-permute-start(bf16[176,1792]{1,0:T(8,128)(2,1)S(1)} %get-tuple-element.485), channel_id=1, source_target_pairs={{0,8},{4,12},{8,0},{12,4},{16,24},{20,28},{24,16},{28,20},{1,9},{5... | collective-permute-start | bytes 1892360 | tf_op jit(solution)/shard_map/while/body/ppermute | solution.py:44
  146.3 29.8 %collective-permute-start.34 = (bf16[176,1792]{1,0:T(8,128)(2,1)S(1)}, bf16[176,1792]{1,0:T(8,128)(2,1)S(1)}, u32[]{:S(2)}, u32[]{:S(2)}) collective-permute-start(bf16[176,1792]{1,0:T(8,128)(2,1)S(1)} %get-tuple-element.486), channel_id=1, source_target_pairs={{0,16},{4,20},{8,24},{12,28},{16,0},{20,4},{24,8},{28,12},{1,17},{... | collective-permute-start | bytes 1892360 | tf_op jit(solution)/shard_map/while/body/ppermute | solution.py:44
  147.8 28.3 %collective-permute-start.35 = (bf16[176,1792]{1,0:T(8,128)(2,1)S(1)}, bf16[176,1792]{1,0:T(8,128)(2,1)S(1)}, u32[]{:S(2)}, u32[]{:S(2)}) collective-permute-start(bf16[176,1792]{1,0:T(8,128)(2,1)S(1)} %get-tuple-element.487), channel_id=1, source_target_pairs={{0,24},{4,28},{8,16},{12,20},{16,8},{20,12},{24,0},{28,4},{1,25},{... | collective-permute-start | bytes 1892360 | tf_op jit(solution)/shard_map/while/body/ppermute | solution.py:44
  151.2 11.8 %collective-permute-start.38 = (bf16[64,1024]{1,0:T(8,128)(2,1)S(1)}, bf16[64,1024]{1,0:T(8,128)(2,1)S(1)}, u32[]{:S(2)}, u32[]{:S(2)}) collective-permute-start(bf16[64,1024]{1,0:T(8,128)(2,1)S(1)} %get-tuple-element.496), channel_id=1, source_target_pairs={{0,2},{1,3},{2,0},{3,1},{4,6},{5,7},{6,4},{7,5},{8,10},{9,11},{10,... | collective-permute-start | bytes 393224 | tf_op jit(solution)/shard_map/while/body/ppermute | solution.py:38
  180.6 20.5 %collective-permute-start.40 = (bf16[176,1280]{1,0:T(8,128)(2,1)S(1)}, bf16[176,1280]{1,0:T(8,128)(2,1)}, u32[]{:S(2)}, u32[]{:S(2)}) collective-permute-start(bf16[176,1280]{1,0:T(8,128)(2,1)S(1)} %get-tuple-element.500), channel_id=1, source_target_pairs={{0,8},{4,12},{8,0},{12,4},{16,24},{20,28},{24,16},{28,20},{1,9},{5... | collective-permute-start | bytes 1351688 | tf_op jit(solution)/shard_map/while/body/ppermute | solution.py:44
  181.8 20.6 %collective-permute-start.41 = (bf16[176,1280]{1,0:T(8,128)(2,1)S(1)}, bf16[176,1280]{1,0:T(8,128)(2,1)}, u32[]{:S(2)}, u32[]{:S(2)}) collective-permute-start(bf16[176,1280]{1,0:T(8,128)(2,1)S(1)} %get-tuple-element.501), channel_id=1, source_target_pairs={{0,16},{4,20},{8,24},{12,28},{16,0},{20,4},{24,8},{28,12},{1,17},{... | collective-permute-start | bytes 1351688 | tf_op jit(solution)/shard_map/while/body/ppermute | solution.py:44
  182.7 19.8 %collective-permute-start.42 = (bf16[176,1280]{1,0:T(8,128)(2,1)S(1)}, bf16[176,1280]{1,0:T(8,128)(2,1)}, u32[]{:S(2)}, u32[]{:S(2)}) collective-permute-start(bf16[176,1280]{1,0:T(8,128)(2,1)S(1)} %get-tuple-element.502), channel_id=1, source_target_pairs={{0,24},{4,28},{8,16},{12,20},{16,8},{20,12},{24,0},{28,4},{1,25},{... | collective-permute-start | bytes 1351688 | tf_op jit(solution)/shard_map/while/body/ppermute | solution.py:44
  184.1 17.0 %collective-permute-start.44 = (bf16[64,1792]{1,0:T(8,128)(2,1)}, bf16[64,1792]{1,0:T(8,128)(2,1)}, u32[]{:S(2)}, u32[]{:S(2)}) collective-permute-start(bf16[64,1792]{1,0:T(8,128)(2,1)} %get-tuple-element.513), channel_id=1, source_target_pairs={{0,2},{1,3},{2,0},{3,1},{4,6},{5,7},{6,4},{7,5},{8,10},{9,11},{10,... | collective-permute-start | bytes 688136 | tf_op jit(solution)/shard_map/while/body/ppermute | solution.py:38
  186.2 14.9 %collective-permute-start.45 = (bf16[64,1792]{1,0:T(8,128)(2,1)}, bf16[64,1792]{1,0:T(8,128)(2,1)}, u32[]{:S(2)}, u32[]{:S(2)}) collective-permute-start(bf16[64,1792]{1,0:T(8,128)(2,1)} %get-tuple-element.514), channel_id=1, source_target_pairs={{0,1},{1,2},{2,3},{3,0},{4,5},{5,6},{6,7},{7,4},{8,9},{9,10},{10,1... | collective-permute-start | bytes 688136 | tf_op jit(solution)/shard_map/while/body/ppermute | solution.py:38
  204.9 12.7 %collective-permute-start.47 = (bf16[64,1280]{1,0:T(8,128)(2,1)S(1)}, bf16[64,1280]{1,0:T(8,128)(2,1)S(1)}, u32[]{:S(2)}, u32[]{:S(2)}) collective-permute-start(bf16[64,1280]{1,0:T(8,128)(2,1)S(1)} %get-tuple-element.520), channel_id=1, source_target_pairs={{0,2},{1,3},{2,0},{3,1},{4,6},{5,7},{6,4},{7,5},{8,10},{9,11},{10,... | collective-permute-start | bytes 491528 | tf_op jit(solution)/shard_map/while/body/ppermute | solution.py:38
  207.6 10.0 %collective-permute-start.48 = (bf16[64,1280]{1,0:T(8,128)(2,1)S(1)}, bf16[64,1280]{1,0:T(8,128)(2,1)S(1)}, u32[]{:S(2)}, u32[]{:S(2)}) collective-permute-start(bf16[64,1280]{1,0:T(8,128)(2,1)S(1)} %get-tuple-element.521), channel_id=1, source_target_pairs={{0,3},{1,0},{2,1},{3,2},{4,7},{5,4},{6,5},{7,6},{8,11},{9,8},{10,9... | collective-permute-start | bytes 491528 | tf_op jit(solution)/shard_map/while/body/ppermute | solution.py:38
  (33 other events, 219.5 us)
